TPU v7x, 128 devices: a whole 4x4x4 slice. The times are simulated.
128 devices in a mesh: row: 16 (over y, z_hi, core), col: 8 (over z_lo, x).
Axes of the slice: x: 4, y: 4, z: 4 (z_hi: 2, z_lo: 2; z = z_hi * 2 + z_lo), core: 2. Of those that a mesh axis runs over, the one named last changes fastest.
Arguments:
- fine_input: bfloat16 [1, 512, 1024, 256], P(None, 'row', 'col'), may hold values from -6 to 6
- coarse_feat: bfloat16 [1, 128, 256, 256], P(None, ('row', 'col')), may hold values from -6 to 6
- conv_weight: bfloat16 [3, 3, 256, 256], replicated, may hold values from -0.125 to 0.125
- step_scale: float32 [1000, 256], replicated, may hold values from 0.5 to 2
- timesteps: int32 [1], replicated, may hold values from 0 to 999
- cotangent: bfloat16 [1, 512, 1024, 256], P(None, 'row', 'col'), may hold values from -6 to 6
Outputs:
- grad_fine: bfloat16 [1, 512, 1024, 256], P(None, 'row', 'col')
- grad_coarse: bfloat16 [1, 128, 256, 256], P(None, ('row', 'col'))
- grad_weight: float32 [3, 3, 256, 256], replicated
All inputs are finite; a program needn't handle non-finite values.
Results may differ from a plain program's by a relative error of at most 0.013.
Values may be sent and summed in bfloat16 or wider, within the bound.
A program may use at most 128 MiB of HBM per device.

v0:
```python
import jax
import jax.numpy as jnp
from jax import lax
from jax.sharding import PartitionSpec as P


def with_halo(block, sides, width):
    for axis, dim in sides:
        count = lax.axis_size(axis)
        forward = [(i, i + 1) for i in range(count - 1)]
        backward = [(target, source) for source, target in forward]
        low = lax.ppermute(
            lax.slice_in_dim(block, block.shape[dim] - width, None, axis=dim), axis, forward
        )
        high = lax.ppermute(lax.slice_in_dim(block, 0, width, axis=dim), axis, backward)
        block = jnp.concatenate([low, block, high], axis=dim)
    return block


def per_device(fine_input, coarse_feat, conv_weight, step_scale, timesteps, cotangent):
    frames, tile_rows, tile_cols, chans = fine_input.shape
    strip = lax.all_gather(coarse_feat, "col", axis=1, tiled=True)
    block = lax.dynamic_slice_in_dim(
        strip, lax.axis_index("col") * (tile_cols // 4), tile_cols // 4, 2
    )
    upper = jnp.repeat(jnp.repeat(block.astype(jnp.float32), 4, axis=1), 4, axis=2)
    hidden = fine_input.astype(jnp.float32) + upper
    sig = jax.nn.sigmoid(hidden)
    act = (hidden * sig).astype(jnp.bfloat16)
    onehot = (
        timesteps[:, None] == jnp.arange(step_scale.shape[0], dtype=jnp.int32)[None, :]
    ).astype(jnp.float32)
    picked = jnp.dot(onehot, step_scale, precision=lax.Precision.HIGHEST)
    dpre = (cotangent.astype(jnp.float32) * picked[:, None, None, :]).astype(jnp.bfloat16)
    pad_act = with_halo(act, (("row", 1), ("col", 2)), 1)
    pad_grad = with_halo(dpre, (("row", 1), ("col", 2)), 1)
    flat_grad = dpre.reshape(-1, chans)
    rows_w = []
    dact = jnp.zeros((frames * tile_rows * tile_cols, chans), jnp.float32)
    for i in range(3):
        taps = []
        for j in range(3):
            window = pad_act[:, i : i + tile_rows, j : j + tile_cols, :].reshape(-1, chans)
            taps.append(
                lax.dot_general(
                    window, flat_grad, (((0,), (0,)), ((), ())), preferred_element_type=jnp.float32
                )
            )
            moved = pad_grad[:, 2 - i : 2 - i + tile_rows, 2 - j : 2 - j + tile_cols, :].reshape(
                -1, chans
            )
            dact = dact + lax.dot_general(
                moved,
                conv_weight[i, j],
                (((1,), (1,)), ((), ())),
                preferred_element_type=jnp.float32,
            )
        rows_w.append(jnp.stack(taps))
    local_weight = jnp.stack(rows_w)
    summed = lax.psum(local_weight, ("row", "col"))
    pixels = frames * tile_rows * lax.axis_size("row") * tile_cols * lax.axis_size("col")
    grad_weight = summed / jnp.sqrt(jnp.float32(pixels))
    dhidden = dact.reshape(frames, tile_rows, tile_cols, chans) * sig * (1.0 + hidden * (1.0 - sig))
    grad_fine = dhidden.astype(jnp.bfloat16)
    pooled = (
        dhidden.reshape(frames, tile_rows // 4, 4, tile_cols // 4, 4, chans)
        .sum(axis=(2, 4))
        .astype(jnp.bfloat16)
    )
    grad_coarse = lax.all_to_all(pooled, "col", split_axis=1, concat_axis=2, tiled=True)
    return (grad_fine, grad_coarse, grad_weight)


def solution(mesh):
    return jax.shard_map(
        per_device,
        mesh=mesh,
        in_specs=(
            P(None, "row", "col", None),
            P(None, ("row", "col"), None, None),
            P(),
            P(),
            P(),
            P(None, "row", "col", None),
        ),
        out_specs=(P(None, "row", "col", None), P(None, ("row", "col"), None, None), P()),
        check_vma=False,
    )
```

profile of v0, /device:TPU:1, one launch (start us, length us, event | category | flops | bytes accessed | tf_op | source)
XLA Modules:
  0.0 290.9 jit_solution(17862606955924848239)
XLA Ops:
  8.0 0.4 copy-done
  8.4 0.4 fusion.87
  8.9 2.0 multiply_convert_fusion.1
  10.9 6.9 %collective-permute-start = (bf16[1,1,128,256]{3,2,1,0:T(8,128)(2,1)S(1)}, bf16[1,1,128,256]{3,2,1,0:T(8,128)(2,1)S(1)}, u32[]{:S(2)}, u32[]{:S(2)}) collective-permute-start(bf16[1,1,128,256]{3,2,1,0:T(8,128)(2,1)S(1)} %get-tuple-element.33), channel_id=1, source_target_pairs={{0,8},{8,16},{16,24},{24,32},{32,40},{40,48},{48,56},{56,64},{64,7... | collective-permute-start | bytes 196616 | tf_op jit(solution)/shard_map/ppermute | solution.py:12
  17.8 1.9 collective-permute-start.1
  19.8 4.1 %copy.19 = bf16[1,32,128,256]{2,3,1,0:T(8,128)(2,1)} copy(bf16[1,32,128,256]{3,2,1,0:T(8,128)(2,1)} %param.6) | data formatting | bytes 4194304 | tf_op args[0]
  23.9 1.0 collective-permute-done.1
  24.9 0.1 pad_maximum_fusion.10
  25.0 1.3 collective-permute-start.2
  26.3 4.1 %collective-permute-start.3 = (bf16[1,34,1,256]{3,2,1,0:T(2,128)(2,1)S(1)}, bf16[1,34,1,256]{3,2,1,0:T(2,128)(2,1)S(1)}, u32[]{:S(2)}, u32[]{:S(2)}) collective-permute-start(bf16[1,34,1,256]{3,2,1,0:T(2,128)(2,1)S(1)} %get-tuple-element.28), channel_id=1, source_target_pairs={{0,1},{1,2},{2,3},{3,4},{4,5},{5,6},{6,7},{8,9},{9,10},{10,11},{11... | collective-permute-start | bytes 52232 | tf_op jit(solution)/shard_map/ppermute | solution.py:12
  30.4 0.3 pad_maximum_fusion.6
  30.7 0.7 fusion.67
  31.5 1.3 pad_maximum_fusion.1
  32.7 4.0 %fusion.82 = (bf16[1,32,128,256]{3,2,1,0:T(8,128)(2,1)S(1)}, bf16[1,32,128,256]{3,2,1,0:T(8,128)(2,1)S(1)}, bf16[1,32,128,256]{3,2,1,0:T(8,128)(2,1)S(1)}, bf16[...) fusion(bf16[1,34,129,256]{3,2,1,0:T(8,128)(2,1)S(1)} %get-tuple-ele, ...), kind=kLoop, calls=%fused_computation.94 | loop fusion | bytes 25165824 | tf_op jit(solution)/shard_map/slice | solution.py:49
  36.8 0.7 convolution_add_fusion.6
  37.5 0.8 convolution_add_fusion.5
  38.3 0.8 convolution_add_fusion.4
  39.1 0.8 convolution_add_fusion.3
  39.9 0.7 fusion.59
  40.6 0.7 convolution_add_fusion.2
  41.4 0.7 convolution_add_fusion.1
  42.1 2.8 fusion
  44.9 5.6 %copy.23 = f32[1,32,128,256]{2,3,1,0:T(8,128)} copy(f32[1,32,128,256]{3,2,1,0:T(8,128)} %bitcast.180) | data formatting | bytes 8388608 | tf_op jit(solution)/shard_map/reshape | solution.py:63
  50.5 4.9 %all-gather.2.cloned.1.call-done = bf16[1,8,256,256]{3,2,0,1:T(8,128)(2,1)} async-done(((bf16[1,1,256,256]{3,2,0,1:T(8,128)(2,1)}), bf16[1,8,256,256]{3,2,0,1:T(8,128)(2,1)}) %all-gather.2.cloned.1.call-update) | async-done | bytes 1048592 | tf_op jit(solution)/shard_map/all_gather | solution.py:22
  55.4 0.9 bitcast_convert_fusion
  56.3 0.2 copy.21
  56.5 1.3 broadcast_in_dim.13
  57.7 2.6 broadcast_in_dim.14
  60.3 3.7 %broadcast_in_dim.15 = f32[32,32,4,256]{3,0,2,1:T(8,128)} broadcast(f32[32,32,256]{2,0,1:T(8,128)} %broadcast_in_dim.14), dimensions={0,1,3} | broadcast | bytes 5242880 | tf_op jit(solution)/shard_map/broadcast_in_dim | solution.py:26
  64.1 5.4 %copy.22 = f32[1,32,128,256]{2,3,1,0:T(8,128)} copy(f32[1,32,128,256]{3,1,2,0:T(8,128)} %bitcast.181) | data formatting | bytes 8388608 | tf_op jit(solution)/shard_map/broadcast_in_dim | solution.py:26
  69.5 6.7 %fusion.81 = (bf16[1,32,128,256]{2,3,1,0:T(8,128)(2,1)}, f32[1,32,128,256]{2,3,1,0:T(8,128)}, bf16[1,32,128,256]{2,3,1,0:T(8,128)(2,1)S(1)}) fusion(f32[1,32,128,256]{2,3,1,0:T(8,128)} %copy.23, f32[1,32,128,256]{2,3,1,0:T(8,128)} %copy.22, bf16[1,32,128,256]{2,3,1,0:T(8,128)(2,1)} %copy.19), kind=kLoop, calls=%fused_computation.93 | loop fusion | flops 13631488 | bytes 18874368 | tf_op jit(solution)/shard_map/convert_element_type | solution.py:64
  76.2 10.0 %collective-permute-start.4 = (bf16[1,1,128,256]{2,3,1,0:T(8,128)(2,1)S(1)}, bf16[1,1,128,256]{2,3,1,0:T(8,128)(2,1)S(1)}, u32[]{:S(2)}, u32[]{:S(2)}) collective-permute-start(bf16[1,1,128,256]{2,3,1,0:T(8,128)(2,1)S(1)} %get-tuple-element.29), channel_id=1, source_target_pairs={{0,8},{8,16},{16,24},{24,32},{32,40},{40,48},{48,56},{56,64},{64,7... | collective-permute-start | bytes 196616 | tf_op jit(solution)/shard_map/ppermute | solution.py:12
  86.2 2.1 collective-permute-start.5
  88.3 0.7 fusion.26
  89.0 4.3 %collective-permute-done.5 = bf16[1,1,128,256]{2,3,1,0:T(8,128)(2,1)S(1)} collective-permute-done((bf16[1,1,128,256]{2,3,1,0:T(8,128)(2,1)S(1)}, bf16[1,1,128,256]{2,3,1,0:T(8,128)(2,1)S(1)}, u32[]{:S(2)}, u32[]{:S(2)}) %collective-permute-start.5) | collective-permute-done | bytes 65568 | tf_op jit(solution)/shard_map/ppermute | solution.py:15
  93.3 0.3 pad_maximum_fusion.3
  93.6 3.0 %fusion.84 = (bf16[1,34,1,256]{2,3,1,0:T(8,128)(2,1)}, bf16[1,34,1,256]{2,3,1,0:T(8,128)(2,1)}) fusion(bf16[1,34,128,256]{2,3,1,0:T(8,128)(2,1)S(1)} %pad_maximum_fusion.3), kind=kLoop, calls=%fused_computation.96 | loop fusion | bytes 69632 | tf_op jit(solution)/shard_map/slice | solution.py:13
  96.6 2.2 copy.25
  98.8 1.3 collective-permute-start.6
  100.1 2.2 copy.27
  102.3 1.4 collective-permute-start.7
  103.7 3.0 %fusion.34 = f32[1,256,256]{2,1,0:T(8,128)} fusion(bf16[1,32,128,256]{3,2,1,0:T(8,128)(2,1)S(1)} %multiply_convert_fusion.1, bf16[1,32,128,256]{2,3,1,0:T(8,128)(2,1)} %copy-done.2, bf16[1,1,128,256]{2,3,1,0:T(8,128)(2,1)S(1)} %collective-permute-done.4), kind=kOutput, calls=%fused_computation.55 | convolution fusion | flops 537919488 | bytes 4521984 | tf_op jit(solution)/shard_map/dot_general | solution.py:45
  106.7 1.4 fusion.51
  108.2 1.9 copy.26
  110.0 1.9 copy.28
  112.0 6.8 %maximum_maximum_fusion = (bf16[1,34,129,256]{2,3,1,0:T(8,128)(2,1)S(1)}, bf16[1,34,129,256]{2,3,1,0:T(8,128)(2,1)S(1)}) fusion(bf16[1,1,128,256]{2,3,1,0:T(8,128)(2,1)S(1)} %collective-permute-done.5, bf16[1,32,128,256]{2,3,1,0:T(8,128)(2,1)} %copy-done.2, bf16[1,1,128,256]{2,3,1,0:T(8,128)(2,1)S(1)} %collective-permute-done.4, ...), kind=kLoop, calls=%fused_computation.8 | loop fusion | flops 17965056 | bytes 6754304 | tf_op jit(solution)/shard_map/concatenate | solution.py:16
  118.8 0.7 fusion.31
  119.5 0.7 fusion.42
  120.2 1.0 fusion.39
  121.3 1.0 fusion.45
  122.3 0.7 fusion.48
  123.0 1.0 fusion.56
  124.2 0.8 copy-done.6
  125.0 0.1 maximum_bitcast_fusion.2
  125.1 1.6 pad_maximum_fusion.2
  126.7 5.7 %copy.24 = f32[1,32,128,256]{3,2,1,0:T(8,128)} copy(f32[1,32,128,256]{2,3,1,0:T(8,128)} %get-tuple-element.13) | data formatting | bytes 8388608 | tf_op jit(solution)/shard_map/mul | solution.py:63
  132.4 5.2 %reshape.132 = f32[8,4,32,4,256]{4,3,2,1,0:T(4,128)} reshape(f32[1,32,128,256]{3,2,1,0:T(8,128)} %copy.24) | data formatting | bytes 8388608 | tf_op jit(solution)/shard_map/reshape | solution.py:66
  137.6 4.3 %reduce_sum.9 = bf16[8,32,256]{2,1,0:T(8,128)(2,1)} reduce(f32[8,4,32,4,256]{4,3,2,1,0:T(4,128)} %reshape.132, f32[]{:T(128)} %constant.6.clone.1), dimensions={1,3}, to_apply=%region_0.0 | reduce | flops 983040 | bytes 4325380 | tf_op jit(solution)/shard_map/reduce_sum | solution.py:67
  141.9 6.3 %all-to-all-start = ((bf16[1,8,32,256]{3,2,0,1:T(8,128)(2,1)}), bf16[1,8,32,256]{3,2,0,1:T(8,128)(2,1)S(1)}, u32[]{:S(2)}, u32[]{:S(2)}) async-start(bf16[1,8,32,256]{3,2,0,1:T(8,128)(2,1)} %bitcast.166), calls=%async_computation | async-start | bytes 262144 | tf_op jit(solution)/shard_map/all_to_all | solution.py:70
  148.2 2.9 copy.29
  151.1 2.5 all-to-all-done
  153.6 126.5 %all-reduce.2.cloned.1.call-done = f32[3,3,256,256]{3,2,1,0:T(8,128)} async-done(((f32[3,3,256,256]{3,2,1,0:T(8,128)}), f32[3,3,256,256]{3,2,1,0:T(8,128)}) %all-reduce.2.cloned.1.call-update) | async-done | bytes 2359312 | tf_op jit(solution)/shard_map/psum | solution.py:60
  280.1 3.3 %broadcast_multiply_fusion = f32[3,3,256,256]{3,2,1,0:T(8,128)} fusion(f32[3,3,256,256]{3,2,1,0:T(8,128)} %all-reduce.2.cloned.1.call-done), kind=kLoop, calls=%fused_computation.52 | loop fusion | flops 589824 | bytes 4718592 | tf_op jit(solution)/shard_map/div | solution.py:62
  283.4 0.7 copy.33
  (30 shorter events, 0.3 us)
Async XLA Ops:
  7.2 1.2 copy-start
  7.2 48.2 %all-gather.2.cloned.1.call-start = ((), (), s32[]{:S(2)}) async-start(), calls=%async_computation.1 | async-start | bytes 1179648 | tf_op jit(solution)/shard_map/all_gather | solution.py:22
  10.9 13.0 %collective-permute-start = (bf16[1,1,128,256]{3,2,1,0:T(8,128)(2,1)S(1)}, bf16[1,1,128,256]{3,2,1,0:T(8,128)(2,1)S(1)}, u32[]{:S(2)}, u32[]{:S(2)}) collective-permute-start(bf16[1,1,128,256]{3,2,1,0:T(8,128)(2,1)S(1)} %get-tuple-element.33), channel_id=1, source_target_pairs={{0,8},{8,16},{16,24},{24,32},{32,40},{40,48},{48,56},{56,64},{64,7... | collective-permute-start | bytes 196616 | tf_op jit(solution)/shard_map/ppermute | solution.py:12
  17.8 7.1 %collective-permute-start.1 = (bf16[1,1,128,256]{3,2,1,0:T(8,128)(2,1)S(1)}, bf16[1,1,128,256]{3,2,1,0:T(8,128)(2,1)S(1)}, u32[]{:S(2)}, u32[]{:S(2)}) collective-permute-start(bf16[1,1,128,256]{3,2,1,0:T(8,128)(2,1)S(1)} %get-tuple-element.34), channel_id=1, source_target_pairs={{8,0},{16,8},{24,16},{32,24},{40,32},{48,40},{56,48},{64,56},{72,6... | collective-permute-start | bytes 196616 | tf_op jit(solution)/shard_map/ppermute | solution.py:15
  19.8 260.4 %all-reduce.2.cloned.1.call-start = ((), (), s32[]{:S(2)}) async-start(), calls=%async_computation.2 | async-start | bytes 4718592 | tf_op jit(solution)/shard_map/psum | solution.py:60
  25.0 6.5 %collective-permute-start.2 = (bf16[1,34,1,256]{3,2,1,0:T(2,128)(2,1)S(1)}, bf16[1,34,1,256]{3,2,1,0:T(2,128)(2,1)S(1)}, u32[]{:S(2)}, u32[]{:S(2)}) collective-permute-start(bf16[1,34,1,256]{3,2,1,0:T(2,128)(2,1)S(1)} %get-tuple-element.27), channel_id=1, source_target_pairs={{1,0},{2,1},{3,2},{4,3},{5,4},{6,5},{7,6},{9,8},{10,9},{11,10},{12... | collective-permute-start | bytes 52232 | tf_op jit(solution)/shard_map/ppermute | solution.py:15
  26.3 4.4 %copy-start.5 = (bf16[3,3,256,256]{3,2,1,0:T(8,128)(2,1)S(1)}, bf16[3,3,256,256]{3,2,1,0:T(8,128)(2,1)}, u32[]{:S(2)}) copy-start(bf16[3,3,256,256]{3,2,1,0:T(8,128)(2,1)} %param.8) | copy-start | bytes 3538948
  26.3 5.2 %collective-permute-start.3 = (bf16[1,34,1,256]{3,2,1,0:T(2,128)(2,1)S(1)}, bf16[1,34,1,256]{3,2,1,0:T(2,128)(2,1)S(1)}, u32[]{:S(2)}, u32[]{:S(2)}) collective-permute-start(bf16[1,34,1,256]{3,2,1,0:T(2,128)(2,1)S(1)} %get-tuple-element.28), channel_id=1, source_target_pairs={{0,1},{1,2},{2,3},{3,4},{4,5},{5,6},{6,7},{8,9},{9,10},{10,11},{11... | collective-permute-start | bytes 52232 | tf_op jit(solution)/shard_map/ppermute | solution.py:12
  76.2 17.1 %copy-start.2 = (bf16[1,32,128,256]{2,3,1,0:T(8,128)(2,1)}, bf16[1,32,128,256]{2,3,1,0:T(8,128)(2,1)S(1)}, u32[]{:S(2)}) copy-start(bf16[1,32,128,256]{2,3,1,0:T(8,128)(2,1)S(1)} %get-tuple-element.14) | copy-start | bytes 6291460
  76.2 12.8 %collective-permute-start.4 = (bf16[1,1,128,256]{2,3,1,0:T(8,128)(2,1)S(1)}, bf16[1,1,128,256]{2,3,1,0:T(8,128)(2,1)S(1)}, u32[]{:S(2)}, u32[]{:S(2)}) collective-permute-start(bf16[1,1,128,256]{2,3,1,0:T(8,128)(2,1)S(1)} %get-tuple-element.29), channel_id=1, source_target_pairs={{0,8},{8,16},{16,24},{24,32},{32,40},{40,48},{48,56},{56,64},{64,7... | collective-permute-start | bytes 196616 | tf_op jit(solution)/shard_map/ppermute | solution.py:12
  86.2 7.1 %collective-permute-start.5 = (bf16[1,1,128,256]{2,3,1,0:T(8,128)(2,1)S(1)}, bf16[1,1,128,256]{2,3,1,0:T(8,128)(2,1)S(1)}, u32[]{:S(2)}, u32[]{:S(2)}) collective-permute-start(bf16[1,1,128,256]{2,3,1,0:T(8,128)(2,1)S(1)} %get-tuple-element.30), channel_id=1, source_target_pairs={{8,0},{16,8},{24,16},{32,24},{40,32},{48,40},{56,48},{64,56},{72,6... | collective-permute-start | bytes 196616 | tf_op jit(solution)/shard_map/ppermute | solution.py:15
  98.8 9.4 %collective-permute-start.6 = (bf16[1,34,1,256]{3,1,2,0:T(8,128)(2,1)S(1)}, bf16[1,34,1,256]{3,1,2,0:T(8,128)(2,1)S(1)}, u32[]{:S(2)}, u32[]{:S(2)}) collective-permute-start(bf16[1,34,1,256]{3,1,2,0:T(8,128)(2,1)S(1)} %copy.25), channel_id=1, source_target_pairs={{0,1},{1,2},{2,3},{3,4},{4,5},{5,6},{6,7},{8,9},{9,10},{10,11},{11... | collective-permute-start | bytes 52232 | tf_op jit(solution)/shard_map/ppermute | solution.py:12
  102.3 4.5 %copy-start.3 = (bf16[1,32,128,256]{2,3,1,0:T(8,128)(2,1)S(1)}, bf16[1,32,128,256]{2,3,1,0:T(8,128)(2,1)}, u32[]{:S(2)}) copy-start(bf16[1,32,128,256]{2,3,1,0:T(8,128)(2,1)} %copy-done.2) | copy-start | bytes 6291460
  102.3 7.8 %collective-permute-start.7 = (bf16[1,34,1,256]{3,1,2,0:T(8,128)(2,1)S(1)}, bf16[1,34,1,256]{3,1,2,0:T(8,128)(2,1)S(1)}, u32[]{:S(2)}, u32[]{:S(2)}) collective-permute-start(bf16[1,34,1,256]{3,1,2,0:T(8,128)(2,1)S(1)} %copy.27), channel_id=1, source_target_pairs={{1,0},{2,1},{3,2},{4,3},{5,4},{6,5},{7,6},{9,8},{10,9},{11,10},{12... | collective-permute-start | bytes 52232 | tf_op jit(solution)/shard_map/ppermute | solution.py:15
  123.0 1.1 copy-start.7
  124.1 1.0 copy-start.6
  137.6 10.6 %copy-start.4 = (bf16[1,32,128,256]{2,3,1,0:T(8,128)(2,1)S(1)}, bf16[1,32,128,256]{2,3,1,0:T(8,128)(2,1)}, u32[]{:S(2)}) copy-start(bf16[1,32,128,256]{2,3,1,0:T(8,128)(2,1)} %get-tuple-element.12) | copy-start | bytes 6291460
  141.9 11.7 %all-to-all-start = ((bf16[1,8,32,256]{3,2,0,1:T(8,128)(2,1)}), bf16[1,8,32,256]{3,2,0,1:T(8,128)(2,1)S(1)}, u32[]{:S(2)}, u32[]{:S(2)}) async-start(bf16[1,8,32,256]{3,2,0,1:T(8,128)(2,1)} %bitcast.166), calls=%async_computation | async-start | bytes 262144 | tf_op jit(solution)/shard_map/all_to_all | solution.py:70
  153.6 130.5 %copy-start.1 = (f32[1000,256]{1,0:T(8,128)S(1)}, f32[1000,256]{1,0:T(8,128)}, u32[]{:S(2)}) copy-start(f32[1000,256]{1,0:T(8,128)} %param.9) | copy-start | bytes 3072004
Sparse Core Ops, SparseCore 0:
  19.9 35.4 all-gather.1
  126.8 153.2 all-reduce.1
where the time goes:
time: 292 us; the launch traced here: 291 us
  waiting for transfers between devices  139 us (48%)
  local copies, waits for them, and re-layouts  53.7 us (18%)
  starting transfers between devices  35.4 us (12%)
  other arithmetic  27.7 us (9%)
  matrix products  19.7 us (7%)
  between operations  15.1 us (5%)
    psum x1, waiting for transfers between devices, per_device(): summed = lax.psum(local_weight, ('row', 'col'))  127 us
    ppermute x4, starting transfers between devices, with_halo(): lax.ppermute(lax.slice_in_dim(block, block.shape[dim] - width, None, axis...  22.3 us
    dot_general x9, matrix products, per_device(): lax.dot_general(window, flat_grad, (((0,), (0,)), ((), ())), preferred_el...  10.4 us
    broadcast_in_dim x2, local copies, waits for them, and re-layouts, per_device(): jnp.repeat(jnp.repeat(block.astype(jnp.float32), 4, axis=1), 4, axis=2)  9.13 us
    unnamed x19, local copies, waits for them, and re-layouts  8.9 us
    dot_general x9, matrix products, per_device(): lax.dot_general(moved, conv_weight[i, j], (((1,), (1,)), ((), ())), prefe...  8.84 us
    concatenate x4, other arithmetic, with_halo(): block = jnp.concatenate([low, block, high], axis=dim)  8.59 us
    ppermute x4, starting transfers between devices, with_halo(): lax.ppermute(lax.slice_in_dim(block, 0, width, axis=dim), axis, backward)  6.74 us
  transfers between devices with their start and end apart: 11, of which 5 were waited for; matrix products, arithmetic and copies ran while one was open for 18% of the time, Pallas kernels for 0%

commit v1 on v0

v1 whole, which is shorter than its diff:
```python
import functools
import math

import jax
import jax.numpy as jnp
from jax import lax
from jax.experimental import pallas as pl
from jax.experimental.pallas import tpu as pltpu
from jax.sharding import PartitionSpec as P

MESH = pl.DeviceIdType.MESH
BF = jnp.bfloat16
F32 = jnp.float32
TN = (((0,), (0,)), ((), ()))
ROWS, COLS, C = 32, 128, 256
PIX = ROWS * COLS
GRID = (16, 8)
STRIPS = 8
PIECE = C // 8


def place(x, y, z, k):
    return (y * 4 + (z // 2) * 2 + k, (z % 2) * 4 + x)


def other(axis, d, flip, x, y, z, k):
    at = [x, y, z]
    at[axis] = (at[axis] + d) % 4
    return place(*at, (k + flip) % 2)


def fused_kernel(
    ts_ref, ss_hbm, fine_hbm, coarse_hbm, w_hbm, cot_hbm,
    gf_ref, gc_ref, gw_ref,
    ss, cot, fine, w, wcat, dcat, act, slope,
    edge32, edge, got_edge, got_row, got_corner, got_coarse, up, patch,
    pool, got_pool, part, stack1, stack2, stack3, whole, pooled_rows,
    load_sem, out_sem, in_sem, pool_out, pool_in, ar_out, ar_in,
):
    row, col = lax.axis_index("row"), lax.axis_index("col")
    y, z, k, x = row // 4, ((row // 2) % 2) * 2 + col // 4, row % 2, col % 4
    here = (x, y, z, k)

    loads = [
        pltpu.make_async_copy(cot_hbm, cot, load_sem.at[0]),
        pltpu.make_async_copy(ss_hbm, ss, load_sem.at[1]),
        pltpu.make_async_copy(w_hbm, w, load_sem.at[2]),
        pltpu.make_async_copy(fine_hbm, fine, load_sem.at[3]),
        pltpu.make_async_copy(
            coarse_hbm.at[pl.ds(col * 32, 32)], got_coarse.at[col], load_sem.at[4]
        ),
    ]

    partners = [(row, (col + d) % 8) for d in range(1, 8)]
    partners += [((row + 1) % 16, col), ((row + 15) % 16, col)]
    partners += [((row + a) % 16, (col + b) % 8) for a in (1, 15) for b in (1, 7)]
    for axis in range(3):
        for d in range(1, 4):
            if axis:
                partners.append(other(axis, d, 0, *here))
            partners.append(other(axis, d, 1, *here))
    barrier = pltpu.get_barrier_semaphore()
    for partner in partners:
        pl.semaphore_signal(barrier, inc=1, device_id=partner, device_id_type=MESH)
    for copy in loads:
        copy.start()

    loads[0].wait()

    def take_edge(r, carry):
        edge32[0, pl.ds(r, 1), :] = cot[r, 0:16, :].astype(F32)[0:1]
        edge32[1, pl.ds(r, 1), :] = cot[r, COLS - 16 : COLS, :].astype(F32)[15:16]
        return carry

    lax.fori_loop(0, ROWS, take_edge, 0, unroll=4)
    edge[...] = edge32[...].astype(BF)

    pl.semaphore_wait(barrier, len(partners))

    def push(src, dst, send, recv, to):
        copy = pltpu.make_async_remote_copy(
            src_ref=src, dst_ref=dst, send_sem=send, recv_sem=recv,
            device_id=to, device_id_type=MESH,
        )
        copy.start()
        return copy

    sent = []
    for d in range(1, 8):
        to = (col + d) % 8
        push(
            coarse_hbm.at[pl.ds(to * 32, 32)], got_coarse.at[col],
            out_sem.at[0], in_sem.at[0], (row, to),
        )
    down, upw, right, left = (row + 1) % 16, (row + 15) % 16, (col + 1) % 8, (col + 7) % 8
    sent.append(push(edge.at[1], got_edge.at[0], out_sem.at[1], in_sem.at[1], (row, right)))
    sent.append(push(edge.at[0], got_edge.at[1], out_sem.at[2], in_sem.at[2], (row, left)))
    sent.append(push(cot_hbm.at[ROWS - 1], got_row.at[0], out_sem.at[3], in_sem.at[3], (down, col)))
    sent.append(push(cot_hbm.at[0], got_row.at[1], out_sem.at[4], in_sem.at[4], (upw, col)))
    for n, (src_row, first, to) in enumerate(
        (
            (ROWS - 1, COLS - 16, (down, right)),
            (ROWS - 1, 0, (down, left)),
            (0, COLS - 16, (upw, right)),
            (0, 0, (upw, left)),
        )
    ):
        sent.append(
            push(
                cot_hbm.at[src_row, pl.ds(first, 16)], got_corner.at[n],
                out_sem.at[5 + n], in_sem.at[5 + n], to,
            )
        )

    loads[1].wait()
    picked = ss[pl.ds(ts_ref[0], 1), :]

    def scaled(raw):
        return (raw.astype(F32) * picked).astype(BF)

    def shift_row(r, carry):
        mid = scaled(cot[r])
        wide = mid.astype(F32)
        at = pl.ds(pl.multiple_of((r + 1) * COLS, COLS), COLS)
        dcat[at, C : 2 * C] = mid
        dcat[at, 2 * C : 3 * C] = pltpu.roll(wide, 1, 0).astype(BF)
        dcat[at, 0:C] = pltpu.roll(wide, COLS - 1, 0).astype(BF)
        return carry

    lax.fori_loop(0, ROWS, shift_row, 0, unroll=2)

    loads[2].wait()
    for i in range(3):
        for j in range(3):
            wcat[i, j * C : (j + 1) * C, :] = w[3 * i + j].T

    keep_top = jnp.where(row > 0, 1.0, 0.0)
    keep_bottom = jnp.where(row < 15, 1.0, 0.0)
    keep_left = jnp.where(col > 0, 1.0, 0.0)
    keep_right = jnp.where(col < 7, 1.0, 0.0)

    for copy in sent:
        copy.wait()
    patch[0] = scaled(got_edge[0]).astype(F32) * keep_left
    patch[1] = scaled(got_edge[1]).astype(F32) * keep_right
    spot = lax.broadcasted_iota(jnp.int32, (16, C), 0)

    def patch_row(r, carry):
        first = pl.ds(pl.multiple_of((r + 1) * COLS, COLS), 16)
        last = pl.ds(pl.multiple_of((r + 1) * COLS + COLS - 16, 16), 16)
        lo = dcat[first, 2 * C : 3 * C].astype(F32)
        dcat[first, 2 * C : 3 * C] = jnp.where(spot == 0, patch[0, pl.ds(r, 1), :], lo).astype(BF)
        hi = dcat[last, 0:C].astype(F32)
        dcat[last, 0:C] = jnp.where(spot == 15, patch[1, pl.ds(r, 1), :], hi).astype(BF)
        return carry

    lax.fori_loop(0, ROWS, patch_row, 0, unroll=4)
    spot_row = lax.broadcasted_iota(jnp.int32, (COLS, C), 0)
    for n, (start, keep) in enumerate(((0, keep_top), ((ROWS + 1) * COLS, keep_bottom))):
        wide = scaled(got_row[n]).astype(F32) * keep
        near = scaled(got_corner[2 * n]).astype(F32)[15:16] * (keep * keep_left)
        far = scaled(got_corner[2 * n + 1]).astype(F32)[0:1] * (keep * keep_right)
        at = pl.ds(start, COLS)
        dcat[at, C : 2 * C] = wide.astype(BF)
        dcat[at, 2 * C : 3 * C] = jnp.where(spot_row == 0, near, pltpu.roll(wide, 1, 0)).astype(BF)
        dcat[at, 0:C] = jnp.where(
            spot_row == COLS - 1, far, pltpu.roll(wide, COLS - 1, 0)
        ).astype(BF)

    loads[3].wait()
    loads[4].wait()
    seven = got_coarse.at[pl.ds(0, 7)]
    pltpu.make_async_copy(seven, seven, in_sem.at[0]).wait()

    def activate(r, carry):
        @pl.when(r % 4 == 0)
        def _():
            coarse = got_coarse[r // 4].astype(F32)
            for n in range(4):
                for half in range(2):
                    up[half, pl.ds(n, 32, stride=4), :] = coarse[:, half * 128 : half * 128 + 128]

        hidden = fine[r].astype(F32) + jnp.concatenate([up[0], up[1]], axis=1)
        sig = 0.5 * jnp.tanh(0.5 * hidden) + 0.5
        value = hidden * sig
        at = pl.ds(pl.multiple_of(r * COLS, COLS), COLS)
        act[at, :] = value.astype(BF)
        slope[at, :] = sig + value * (1.0 - sig)
        return carry

    lax.fori_loop(0, ROWS, activate, 0)

    def order(j):
        return ((0, 1, 2), (1, 2, 0), (2, 0, 1))[j]

    def mine(j):
        return here[order(j)[0]] * 2 + k

    def group(j):
        axis = order(j)[0]
        return [
            (d, flip, ((here[axis] + d) % 4) * 2 + (k + flip) % 2, other(axis, d, flip, *here))
            for d in range(4)
            for flip in range(2)
            if d or flip
        ]

    def taps(i, carry):
        at = pl.ds(pl.multiple_of((2 - i) * COLS, COLS), PIX)
        for j in range(3):
            t = i * 3 + j
            part[t] = lax.dot_general(
                act[...], dcat[at, j * C : (j + 1) * C], TN, preferred_element_type=F32
            ).astype(BF)
            for _, _, m, to in group(j):
                push(
                    part.at[t, pl.ds(m * PIECE, PIECE)], stack1.at[t, mine(j)],
                    ar_out.at[0, t], ar_in.at[0, t], to,
                )
            stack1[t, mine(j)] = part[t, pl.ds(pl.multiple_of(mine(j) * PIECE, PIECE), PIECE), :]
        return carry

    lax.fori_loop(0, 3, taps, 0)

    def total(stack, t, count):
        out = stack[t, 0].astype(F32)
        for n in range(1, count):
            out = out + stack[t, n].astype(F32)
        return out.astype(BF)

    def arrived(stack, t, count, sem):
        some = stack.at[t, pl.ds(0, count)]
        pltpu.make_async_copy(some, some, sem).wait()

    def exchange(stack, t, j, phase):
        axis = order(j)[phase]
        for d in range(1, 4):
            push(
                stack.at[t, here[axis]], stack.at[t, here[axis]],
                ar_out.at[phase, t], ar_in.at[phase, t], other(axis, d, 0, *here),
            )

    def step1(i):
        for j in range(3):
            t = i * 3 + j
            arrived(stack1, t, 7, ar_in.at[0, t])
            stack2[t, here[order(j)[1]]] = total(stack1, t, 8)
            exchange(stack2, t, j, 1)

    def step2(i):
        for j in range(3):
            t = i * 3 + j
            arrived(stack2, t, 3, ar_in.at[1, t])
            stack3[t, here[order(j)[2]]] = total(stack2, t, 4)
            exchange(stack3, t, j, 2)

    def step3(i):
        for j in range(3):
            t = i * 3 + j
            arrived(stack3, t, 3, ar_in.at[2, t])
            at = pl.ds(pl.multiple_of(mine(j) * PIECE, PIECE), PIECE)
            whole[t, at, :] = total(stack3, t, 4)
            for _, _, _, to in group(j):
                push(whole.at[t, at], whole.at[t, at], ar_out.at[3, t], ar_in.at[3, t], to)

    scale = 1.0 / math.sqrt(PIX * GRID[0] * GRID[1])

    def step4(i):
        for j in range(3):
            t = i * 3 + j
            some = whole.at[t, pl.ds(0, 7 * PIECE)]
            pltpu.make_async_copy(some, some, ar_in.at[3, t]).wait()
            gw_ref[t] = whole[t].astype(F32) * scale

    def strip(n, carry):
        c = (col + 1 + n) % 8
        base = c * (4 * COLS)
        acc = None
        for i in range(3):
            at = pl.ds(pl.multiple_of(base + (2 - i) * COLS, COLS), 4 * COLS)
            term = jnp.dot(dcat[at, :], wcat[i], preferred_element_type=F32)
            acc = term if acc is None else acc + term
        at = pl.ds(pl.multiple_of(base, COLS), 4 * COLS)
        dh = acc * slope[at, :]
        gf_ref[at, :] = dh.astype(BF)
        tall = dh[0:COLS] + dh[COLS : 2 * COLS] + dh[2 * COLS : 3 * COLS] + dh[3 * COLS :]
        for half in range(2):
            lanes = slice(half * 128, half * 128 + 128)
            pooled_rows[half] = tall[:, lanes]
            cells = pooled_rows[half, pl.ds(0, 32, stride=4), :]
            for q in range(1, 4):
                cells = cells + pooled_rows[half, pl.ds(q, 32, stride=4), :]
            pool[n, :, lanes] = cells.astype(BF)
        slot = pl.ds(pl.multiple_of(col * 32, 32), 32)

        @pl.when(n < 7)
        def _():
            push(pool.at[n], got_pool.at[slot], pool_out, pool_in, (row, c))

        @pl.when(n == 7)
        def _():
            got_pool[slot, :] = pool[n]

        return carry

    plan = (
        (1, [(step1, 0)]),
        (3, [(step1, 1)]),
        (5, [(step2, 0), (step1, 2)]),
        (7, [(step2, 1)]),
        (8, [(step3, 0), (step2, 2), (step3, 1), (step3, 2)]),
    )
    done = 0
    for until, steps in plan:
        lax.fori_loop(done, until, strip, 0)
        done = until
        for step, i in steps:
            step(i)

    some = got_pool.at[pl.ds(0, 7 * 32)]
    pltpu.make_async_copy(some, some, pool_in).wait()
    gc_ref[...] = got_pool[...]
    for i in range(3):
        step4(i)

    seven = pool.at[pl.ds(0, 7)]
    pltpu.make_async_copy(seven, seven, pool_out).wait()
    seven = got_coarse.at[pl.ds(0, 7)]
    pltpu.make_async_copy(seven, seven, out_sem.at[0]).wait()
    for t in range(9):
        for phase, count in ((0, 7), (1, 3), (2, 3), (3, 7)):
            some = stack1.at[t, pl.ds(0, count)]
            pltpu.make_async_copy(some, some, ar_out.at[phase, t]).wait()


def store_kernel(gf_ref, gc_ref, gw_ref, gf_out, gc_out, gw_out, sem):
    copies = [
        pltpu.make_async_copy(src, dst, sem.at[n])
        for n, (src, dst) in enumerate(((gw_ref, gw_out), (gf_ref, gf_out), (gc_ref, gc_out)))
    ]
    for copy in copies:
        copy.start()
    for copy in copies:
        copy.wait()


def per_device(fine_input, coarse_feat, conv_weight, step_scale, timesteps, cotangent):
    anywhere = pl.BlockSpec(memory_space=pl.ANY)
    vmem = pl.BlockSpec(memory_space=pltpu.VMEM)
    buf = pltpu.VMEM
    dma = pltpu.SemaphoreType.DMA
    results = pl.pallas_call(
        fused_kernel,
        name="fused",
        out_shape=(
            pltpu.VMEM((PIX, C), BF),
            pltpu.VMEM((C, C), BF),
            pltpu.VMEM((9, C, C), F32),
        ),
        in_specs=[pl.BlockSpec(memory_space=pltpu.SMEM)] + [anywhere] * 5,
        out_specs=(vmem, vmem, vmem),
        scratch_shapes=[
            buf((1000, C), F32),
            buf((ROWS, COLS, C), BF),
            buf((ROWS, COLS, C), BF),
            buf((9, C, C), BF),
            buf((3, 3 * C, C), BF),
            buf(((ROWS + 2) * COLS, 3 * C), BF),
            buf((PIX, C), BF),
            buf((PIX, C), F32),
            buf((2, ROWS, C), F32),
            buf((2, ROWS, C), BF),
            buf((2, ROWS, C), BF),
            buf((2, COLS, C), BF),
            buf((4, 16, C), BF),
            buf((8, 32, C), BF),
            buf((2, COLS, 128), F32),
            buf((2, ROWS, C), F32),
            buf((8, 32, C), BF),
            buf((C, C), BF),
            buf((9, C, C), BF),
            buf((9, 8, PIECE, C), BF),
            buf((9, 4, PIECE, C), BF),
            buf((9, 4, PIECE, C), BF),
            buf((9, C, C), BF),
            buf((2, COLS, 128), F32),
            dma((5,)),
            dma((9,)),
            dma((9,)),
            dma,
            dma,
            dma((4, 9)),
            dma((4, 9)),
        ],
        compiler_params=pltpu.CompilerParams(
            collective_id=0, has_side_effects=True, vmem_limit_bytes=48 * 2**20
        ),
        cost_estimate=pl.CostEstimate(
            flops=2 * 2 * 9 * PIX * C * C, bytes_accessed=12 * 2**20, transcendentals=PIX * C
        ),
    )(
        timesteps,
        step_scale,
        fine_input.reshape(ROWS, COLS, C),
        coarse_feat.reshape(C, C),
        conv_weight.reshape(9, C, C),
        cotangent.reshape(ROWS, COLS, C),
    )
    gf, gc, gw = pl.pallas_call(
        store_kernel,
        name="store",
        out_shape=(
            jax.ShapeDtypeStruct((PIX, C), BF),
            jax.ShapeDtypeStruct((C, C), BF),
            jax.ShapeDtypeStruct((9, C, C), F32),
        ),
        in_specs=[vmem] * 3,
        out_specs=(anywhere, anywhere, anywhere),
        scratch_shapes=[dma((3,))],
    )(*results)
    return gf.reshape(1, ROWS, COLS, C), gc.reshape(1, 1, C, C), gw.reshape(3, 3, C, C)


def solution(mesh):
    return jax.shard_map(
        per_device,
        mesh=mesh,
        in_specs=(
            P(None, "row", "col", None),
            P(None, ("row", "col"), None, None),
            P(),
            P(),
            P(),
            P(None, "row", "col", None),
        ),
        out_specs=(P(None, "row", "col", None), P(None, ("row", "col"), None, None), P()),
        check_vma=False,
    )
```

time: 292 us -> 58.2 us (0.20)
  waiting for transfers between devices: 139 us -> 0 us
  Pallas kernels: 0 us -> 51.2 us
  local copies, waits for them, and re-layouts: 53.7 us -> 5.48 us
  starting transfers between devices: 35.4 us -> 0 us
  other arithmetic: 27.7 us -> 0 us
  matrix products: 19.7 us -> 0 us
  between operations: 15.1 us -> 1.31 us
    psum x1 -> x0, waiting for transfers between devices: 127 us -> none  [per_device(): summed = lax.psum(local_weight, ('row', 'col'))]
    pallas_call x0 -> x2, Pallas kernels: none -> 51.2 us  [the longest x1 46.7 us: per_device(): pl.pallas_call(fused_kernel, name='fused', out_shape=(pltpu.VMEM((PIX, C)...]
    ppermute x8 -> x0, starting transfers between devices: 29 us -> none  [the longest x4 22.3 us: with_halo(): lax.ppermute(lax.slice_in_dim(block, block.shape[dim] - width, None, axis...]
    dot_general x19 -> x0, matrix products: 19.7 us -> none  [the longest x9 10.4 us: per_device(): lax.dot_general(window, flat_grad, (((0,), (0,)), ((), ())), preferred_el...]
    broadcast_in_dim x4 -> x0, local copies, waits for them, and re-layouts: 13 us -> none  [the longest x2 9.13 us: per_device(): jnp.repeat(jnp.repeat(block.astype(jnp.float32), 4, axis=1), 4, axis=2)]
    slice x6 -> x0, local copies, waits for them, and re-layouts: 11.4 us -> none  [the longest x4 5.23 us: with_halo(): lax.slice_in_dim(block, block.shape[dim] - width, None, axis=dim)]
    reshape x2 -> x0, local copies, waits for them, and re-layouts: 10.7 us -> none  [the longest x1 5.59 us: per_device(): dact.reshape(frames, tile_rows, tile_cols, chans) * sig]
    convert_element_type x3 -> x0, other arithmetic: 9.7 us -> none  [the longest x1 6.73 us: per_device(): grad_fine = dhidden.astype(jnp.bfloat16)]
  transfers between devices with their start and end apart: 11 -> 0, of which waited for: 5 -> 0; matrix products, arithmetic and copies ran while one was open for 18% -> 0% of each run, Pallas kernels for 0% -> 0%
where the time goes in v1:
time: 58.2 us; the launch traced here: 58 us
  Pallas kernels  51.2 us (88%)
  local copies, waits for them, and re-layouts  5.48 us (9%)
  between operations  1.31 us (2%)
    pallas_call x1, Pallas kernels, per_device(): pl.pallas_call(fused_kernel, name='fused', out_shape=(pltpu.VMEM((PIX, C)...  46.7 us
    unnamed x10, local copies, waits for them, and re-layouts  5.48 us
    pallas_call x1, Pallas kernels, per_device(): pl.pallas_call(store_kernel, name='store', out_shape=(jax.ShapeDtypeStruc...  4.52 us

profile of v1, /device:TPU:1, one launch (start us, length us, event | category | flops | bytes accessed | tf_op | source)
XLA Modules:
  0.0 58.0 jit_solution(15305576441213397442)
XLA Ops:
  1.3 0.0 copy-start.3
  1.3 1.2 %copy-done.3 = f32[1000,256]{1,0:T(8,128)S(1)} copy-done((f32[1000,256]{1,0:T(8,128)S(1)}, f32[1000,256]{1,0:T(8,128)}, u32[]{:S(2)}) %copy-start.3) | copy-done | bytes 1024024
  2.5 0.0 copy-start.4
  2.5 0.9 %copy-done.4 = bf16[1,1,256,256]{3,2,1,0:T(8,128)(2,1)S(1)} copy-done((bf16[1,1,256,256]{3,2,1,0:T(8,128)(2,1)S(1)}, bf16[1,1,256,256]{3,2,1,0:T(8,128)(2,1)}, u32[]{:S(2)}) %copy-start.4) | copy-done | bytes 131096
  3.4 46.7 %fused.1 = (bf16[4096,256]{1,0:T(8,128)(2,1)S(1)}, bf16[256,256]{1,0:T(8,128)(2,1)S(1)}, f32[9,256,256]{2,1,0:T(8,128)S(1)}) custom-call(s32[1]{0:T(128)S(6)} %copy.9.ts_ref, f32[1000,256]{1,0:T(8,128)S(1)} %copy-done.3, bf16[32,128,256]{2,1,0:T(8,128)(2,1)} %bitcast.9, bf16[256,256]{1,0:T(8,128)(2,1)S(1)} %bitcast.7, bf16[9,256,256]{2,1,0:T(8,128)(2,1)} %bitcast.12, ...), custom_call_target="tpu_custom_call" | custom-call | flops 9663676416 | bytes 12582912 | tf_op jit(solution)/shard_map/fused/pallas_call | solution.py:352
  50.1 0.0 copy-start
  50.1 1.4 %copy-done = f32[9,256,256]{2,1,0:T(8,128)} copy-done((f32[9,256,256]{2,1,0:T(8,128)}, f32[9,256,256]{2,1,0:T(8,128)S(1)}, u32[]{:S(2)}) %copy-start) | copy-done | bytes 2359320
  51.5 0.0 copy-start.1
  51.5 1.3 %copy-done.1 = bf16[4096,256]{1,0:T(8,128)(2,1)} copy-done((bf16[4096,256]{1,0:T(8,128)(2,1)}, bf16[4096,256]{1,0:T(8,128)(2,1)S(1)}, u32[]{:S(2)}) %copy-start.1) | copy-done | bytes 2097176
  52.8 0.0 copy-start.2
  52.8 0.7 %copy-done.2 = bf16[256,256]{1,0:T(8,128)(2,1)} copy-done((bf16[256,256]{1,0:T(8,128)(2,1)}, bf16[256,256]{1,0:T(8,128)(2,1)S(1)}, u32[]{:S(2)}) %copy-start.2) | copy-done | bytes 131096
  53.5 4.5 %store.1 = (bf16[4096,256]{1,0:T(8,128)(2,1)}, bf16[256,256]{1,0:T(8,128)(2,1)}, f32[9,256,256]{2,1,0:T(8,128)}) custom-call(bf16[4096,256]{1,0:T(8,128)(2,1)} %copy-done.1, bf16[256,256]{1,0:T(8,128)(2,1)} %copy-done.2, f32[9,256,256]{2,1,0:T(8,128)} %copy-done), custom_call_target="tpu_custom_call" | custom-call | tf_op jit(solution)/shard_map/store/pallas_call | solution.py:409
Async XLA Ops:
  1.3 1.2 %copy-start.3 = (f32[1000,256]{1,0:T(8,128)S(1)}, f32[1000,256]{1,0:T(8,128)}, u32[]{:S(2)}) copy-start(f32[1000,256]{1,0:T(8,128)} %ss_hbm.1) | copy-start | bytes 3072004
  2.5 0.9 %copy-start.4 = (bf16[1,1,256,256]{3,2,1,0:T(8,128)(2,1)S(1)}, bf16[1,1,256,256]{3,2,1,0:T(8,128)(2,1)}, u32[]{:S(2)}) copy-start(bf16[1,1,256,256]{3,2,1,0:T(8,128)(2,1)} %param.7) | copy-start | bytes 393220
  50.1 1.4 %copy-start = (f32[9,256,256]{2,1,0:T(8,128)}, f32[9,256,256]{2,1,0:T(8,128)S(1)}, u32[]{:S(2)}) copy-start(f32[9,256,256]{2,1,0:T(8,128)S(1)} %get-tuple-element.11.gw_ref) | copy-start | bytes 7077892
  51.5 1.3 %copy-start.1 = (bf16[4096,256]{1,0:T(8,128)(2,1)}, bf16[4096,256]{1,0:T(8,128)(2,1)S(1)}, u32[]{:S(2)}) copy-start(bf16[4096,256]{1,0:T(8,128)(2,1)S(1)} %get-tuple-element.9.gf_ref) | copy-start | bytes 6291460
  52.8 0.7 %copy-start.2 = (bf16[256,256]{1,0:T(8,128)(2,1)}, bf16[256,256]{1,0:T(8,128)(2,1)S(1)}, u32[]{:S(2)}) copy-start(bf16[256,256]{1,0:T(8,128)(2,1)S(1)} %get-tuple-element.10.gc_ref) | copy-start | bytes 393220

commit v2 on v1

v2 whole, which is shorter than its diff:
```python
import functools
import math

import jax
import jax.numpy as jnp
from jax import lax
from jax.experimental import pallas as pl
from jax.experimental.pallas import tpu as pltpu
from jax.sharding import PartitionSpec as P

MESH = pl.DeviceIdType.MESH
BF = jnp.bfloat16
F32 = jnp.float32
ROWS, COLS, C = 32, 128, 256
PIX = ROWS * COLS
GRID = (16, 8)
STRIPS = 8
PIECE = C // 8
HALF = C // 2
WHEN = ((1, 2, 3), (4, 6, 7), (8, 10, 11), (12, 13, 14), (15, 16, 17), (16, 17, 18))


def place(x, y, z, k):
    return (y * 4 + (z // 2) * 2 + k, (z % 2) * 4 + x)


def other(axis, d, flip, x, y, z, k):
    at = [x, y, z]
    at[axis] = (at[axis] + d) % 4
    return place(*at, (k + flip) % 2)


def fused_kernel(
    ts_ref, ss_hbm, fine_hbm, coarse_hbm, w_hbm, cot_hbm,
    gf_ref, gc_ref, gw_ref,
    ss, cot, fine, w, wcat, dcat, act_t, slope,
    edge32, edge, got_edge, got_row, got_corner, got_coarse, up, patch,
    pool, got_pool, part, pair, half_sum, stack1, stack2, stack3, whole, pooled_rows,
    load_sem, out_sem, in_sem, coarse_out, coarse_in, pool_out, pool_in, ar_out, ar_in,
):
    row, col = lax.axis_index("row"), lax.axis_index("col")
    y, z_hi, k, z_lo, x = row // 4, (row // 2) % 2, row % 2, col // 4, col % 4
    z = z_hi * 2 + z_lo
    here = (x, y, z, k)
    twin = place(x, y, z, 1 - k)

    down, upw, right, left = (row + 1) % 16, (row + 15) % 16, (col + 1) % 8, (col + 7) % 8
    partners = [(row, (col + d) % 8) for d in range(1, 8)]
    partners += [(down, col), (upw, col)]
    partners += [(a, b) for a in (down, upw) for b in (left, right)]
    partners += [other(1, d, 0, *here) for d in range(1, 4)]
    partners += [place(x, y, (z + 2) % 4, k), place(x, y, 3 - z, k)]
    barrier = pltpu.get_barrier_semaphore()
    for partner in partners:
        pl.semaphore_signal(barrier, inc=1, device_id=partner, device_id_type=MESH)

    loads = [
        pltpu.make_async_copy(cot_hbm, cot, load_sem.at[0]),
        pltpu.make_async_copy(ss_hbm, ss, load_sem.at[1]),
        pltpu.make_async_copy(w_hbm, w, load_sem.at[2]),
        pltpu.make_async_copy(fine_hbm, fine, load_sem.at[3]),
        pltpu.make_async_copy(
            coarse_hbm.at[pl.ds(col * 32, 32)], got_coarse.at[col], load_sem.at[4]
        ),
    ]
    for copy in loads:
        copy.start()

    loads[0].wait()

    def take_edge(r, carry):
        edge32[0, pl.ds(r, 1), :] = cot[r, 0:16, :].astype(F32)[0:1]
        edge32[1, pl.ds(r, 1), :] = cot[r, COLS - 16 : COLS, :].astype(F32)[15:16]
        return carry

    lax.fori_loop(0, ROWS, take_edge, 0, unroll=8)
    edge[...] = edge32[...].astype(BF)

    pl.semaphore_wait(barrier, len(partners))

    def push(src, dst, send, recv, to):
        copy = pltpu.make_async_remote_copy(
            src_ref=src, dst_ref=dst, send_sem=send, recv_sem=recv,
            device_id=to, device_id_type=MESH,
        )
        copy.start()
        return copy

    def near_strip(n):
        m = n % 4
        return ((z_lo + n // 4) % 2) * 4 + (x + (m * (m + 1) // 2)) % 4

    for n in range(7, 0, -1):
        to = near_strip(n)
        push(
            coarse_hbm.at[pl.ds(to * 32, 32)], got_coarse.at[col],
            coarse_out, coarse_in.at[col], (row, to),
        )
    sent = []
    for n, (src_row, first, to) in enumerate(
        (
            (ROWS - 1, COLS - 16, (down, right)),
            (ROWS - 1, 0, (down, left)),
            (0, COLS - 16, (upw, right)),
            (0, 0, (upw, left)),
        )
    ):
        sent.append(
            push(
                cot_hbm.at[src_row, pl.ds(first, 16)], got_corner.at[n],
                out_sem.at[n], in_sem.at[n], to,
            )
        )
    sent.append(push(cot_hbm.at[ROWS - 1], got_row.at[0], out_sem.at[4], in_sem.at[4], (down, col)))
    sent.append(push(cot_hbm.at[0], got_row.at[1], out_sem.at[5], in_sem.at[5], (upw, col)))
    sent.append(push(edge.at[1], got_edge.at[0], out_sem.at[6], in_sem.at[6], (row, right)))
    sent.append(push(edge.at[0], got_edge.at[1], out_sem.at[7], in_sem.at[7], (row, left)))

    loads[1].wait()
    picked = ss[pl.ds(ts_ref[0], 1), :]

    def scaled(raw):
        return (raw.astype(F32) * picked).astype(BF)

    def shift_row(r, carry):
        mid = scaled(cot[r])
        wide = mid.astype(F32)
        at = pl.ds(pl.multiple_of((r + 1) * COLS, COLS), COLS)
        dcat[at, C : 2 * C] = mid
        dcat[at, 2 * C : 3 * C] = pltpu.roll(wide, 1, 0).astype(BF)
        dcat[at, 0:C] = pltpu.roll(wide, COLS - 1, 0).astype(BF)
        return carry

    lax.fori_loop(0, ROWS, shift_row, 0, unroll=2)

    loads[2].wait()

    def turn_weight(i, carry):
        for j in range(3):
            wcat[i, j * C : (j + 1) * C, :] = w[3 * i + j].T
        return carry

    lax.fori_loop(0, 3, turn_weight, 0)

    loads[3].wait()
    loads[4].wait()

    def activate(n, carry):
        strip = near_strip(n)

        @pl.when(n > 0)
        def _():
            some = got_coarse.at[strip]
            pltpu.make_async_copy(some, some, coarse_in.at[strip]).wait()

        coarse = got_coarse[strip].astype(F32)
        for q in range(4):
            for half in range(2):
                up[half, pl.ds(q, 32, stride=4), :] = coarse[:, half * 128 : half * 128 + 128]

        def fine_row(q, carry):
            r = strip * 4 + q
            hidden = fine[r].astype(F32) + jnp.concatenate([up[0], up[1]], axis=1)
            sig = 0.5 * jnp.tanh(0.5 * hidden) + 0.5
            value = hidden * sig
            at = pl.ds(pl.multiple_of(r * COLS, COLS), COLS)
            act_t[:, at] = value.astype(BF).T
            slope[at, :] = sig + value * (1.0 - sig)
            return carry

        return lax.fori_loop(0, 4, fine_row, carry, unroll=2)

    lax.fori_loop(0, STRIPS, activate, 0)

    keep_top = jnp.where(row > 0, 1.0, 0.0)
    keep_bottom = jnp.where(row < 15, 1.0, 0.0)
    keep_left = jnp.where(col > 0, 1.0, 0.0)
    keep_right = jnp.where(col < 7, 1.0, 0.0)

    for copy in sent:
        copy.wait()
    patch[0] = scaled(got_edge[0]).astype(F32) * keep_left
    patch[1] = scaled(got_edge[1]).astype(F32) * keep_right
    spot = lax.broadcasted_iota(jnp.int32, (16, C), 0)

    def patch_row(r, carry):
        first = pl.ds(pl.multiple_of((r + 1) * COLS, COLS), 16)
        last = pl.ds(pl.multiple_of((r + 1) * COLS + COLS - 16, 16), 16)
        lo = dcat[first, 2 * C : 3 * C].astype(F32)
        dcat[first, 2 * C : 3 * C] = jnp.where(spot == 0, patch[0, pl.ds(r, 1), :], lo).astype(BF)
        hi = dcat[last, 0:C].astype(F32)
        dcat[last, 0:C] = jnp.where(spot == 15, patch[1, pl.ds(r, 1), :], hi).astype(BF)
        return carry

    lax.fori_loop(0, ROWS, patch_row, 0, unroll=4)
    spot_row = lax.broadcasted_iota(jnp.int32, (COLS, C), 0)
    for n, (start, keep) in enumerate(((0, keep_top), ((ROWS + 1) * COLS, keep_bottom))):
        wide = scaled(got_row[n]).astype(F32) * keep
        near = scaled(got_corner[2 * n]).astype(F32)[15:16] * (keep * keep_left)
        far = scaled(got_corner[2 * n + 1]).astype(F32)[0:1] * (keep * keep_right)
        at = pl.ds(start, COLS)
        dcat[at, C : 2 * C] = wide.astype(BF)
        dcat[at, 2 * C : 3 * C] = jnp.where(spot_row == 0, near, pltpu.roll(wide, 1, 0)).astype(BF)
        dcat[at, 0:C] = jnp.where(
            spot_row == COLS - 1, far, pltpu.roll(wide, COLS - 1, 0)
        ).astype(BF)

    my_half = pl.ds(pl.multiple_of(k * HALF, HALF), HALF)
    twin_half = pl.ds(pl.multiple_of((1 - k) * HALF, HALF), HALF)

    def one_hot(axis):
        return (1 - axis) * (2 - axis) // 2, axis * (2 - axis), axis * (axis - 1) // 2

    def mine(axis):
        a, b, c = one_hot(axis)
        return a * x + b * y + c * z

    def peers(axis):
        a, b, c = one_hot(axis)
        me = mine(axis)
        for d in range(1, 4):
            yield (me + d) % 4, place((x + d * a) % 4, (y + d * b) % 4, (z + d * c) % 4, k)

    def arrived(some, sem):
        pltpu.make_async_copy(some, some, sem).wait()

    def total(stack, t):
        out = stack[t, 0].astype(F32)
        for n in range(1, 4):
            out = out + stack[t, n].astype(F32)
        return out.astype(BF)

    def quarter(m):
        return pl.ds(pl.multiple_of(m * PIECE, PIECE), PIECE)

    def step0(t, j):
        arrived(pair.at[t], ar_in.at[0, t])
        half_sum[t] = (part[t, my_half, :].astype(F32) + pair[t].astype(F32)).astype(BF)
        me = mine(j)
        for m, to in peers(j):
            push(half_sum.at[t, quarter(m)], stack1.at[t, me], ar_out.at[1, t], ar_in.at[1, t], to)
        stack1[t, me] = half_sum[t, quarter(me), :]

    def exchange(before, after, phase):
        def step(t, j):
            arrived(before.at[t, pl.ds(0, 3)], ar_in.at[phase, t])
            axis = (j + phase) % 3
            me = mine(axis)
            after[t, me] = total(before, t)
            for _, to in peers(axis):
                push(
                    after.at[t, me], after.at[t, me],
                    ar_out.at[phase + 1, t], ar_in.at[phase + 1, t], to,
                )

        return step

    def step3(t, j):
        arrived(stack3.at[t, pl.ds(0, 3)], ar_in.at[3, t])
        at = quarter(4 * k + mine(j))
        whole[t, at, :] = total(stack3, t)
        for _, to in peers(j):
            push(whole.at[t, at], whole.at[t, at], ar_out.at[4, t], ar_in.at[4, t], to)

    def step4(t, j):
        arrived(whole.at[t, pl.ds(0, 3 * PIECE)], ar_in.at[4, t])
        push(whole.at[t, my_half], whole.at[t, my_half], ar_out.at[5, t], ar_in.at[5, t], twin)

    scale = 1.0 / math.sqrt(PIX * GRID[0] * GRID[1])

    def step5(t, j):
        arrived(whole.at[t, pl.ds(0, HALF)], ar_in.at[5, t])
        gw_ref[t] = whole[t].astype(F32) * scale

    def first_tap(g):
        return 3 * ((4 - g) % 3)

    def taps(g):
        first = first_tap(g)
        at = pl.ds(pl.multiple_of(2 * COLS - first // 3 * COLS, COLS), PIX)
        for j in range(3):
            part[first + j] = jnp.dot(
                act_t[...], dcat[at, j * C : (j + 1) * C], preferred_element_type=F32
            ).astype(BF)
        for j in range(3):
            t = first + j
            push(part.at[t, twin_half], pair.at[t], ar_out.at[0, t], ar_in.at[0, t], twin)

    def strip(n):
        c = (col + 1 + n) % 8
        base = c * (4 * COLS)
        acc = None
        for i in range(3):
            at = pl.ds(pl.multiple_of(base + (2 - i) * COLS, COLS), 4 * COLS)
            term = jnp.dot(dcat[at, :], wcat[i], preferred_element_type=F32)
            acc = term if acc is None else acc + term
        at = pl.ds(pl.multiple_of(base, COLS), 4 * COLS)
        dh = acc * slope[at, :]
        gf_ref[at, :] = dh.astype(BF)
        tall = dh[0:COLS] + dh[COLS : 2 * COLS] + dh[2 * COLS : 3 * COLS] + dh[3 * COLS :]
        for half in range(2):
            lanes = slice(half * 128, half * 128 + 128)
            pooled_rows[half] = tall[:, lanes]
            cells = pooled_rows[half, pl.ds(0, 32, stride=4), :]
            for q in range(1, 4):
                cells = cells + pooled_rows[half, pl.ds(q, 32, stride=4), :]
            pool[n, :, lanes] = cells.astype(BF)
        slot = pl.ds(pl.multiple_of(col * 32, 32), 32)

        @pl.when(n < 7)
        def _():
            push(pool.at[n], got_pool.at[slot], pool_out, pool_in, (row, c))

        @pl.when(n == 7)
        def _():
            got_pool[slot, :] = pool[n]

    steps = (step0, exchange(stack1, stack2, 1), exchange(stack2, stack3, 2), step3, step4, step5)

    def slot(u, carry):
        @pl.when(u < 3)
        def _():
            taps(u)

        @pl.when((u >= 3) & (u < 3 + STRIPS))
        def _():
            strip(u - 3)

        for step, (first, second, third) in zip(steps, WHEN):
            @pl.when((u == first) | (u == second) | (u == third))
            def _():
                g = jnp.where(u == first, 0, jnp.where(u == second, 1, 2))
                lax.fori_loop(0, 3, lambda j, c: (step(first_tap(g) + j, j), c)[1], 0)

        return carry

    lax.fori_loop(0, WHEN[-1][-1] + 1, slot, 0)

    arrived(got_pool.at[pl.ds(0, 7 * 32)], pool_in)
    gc_ref[...] = got_pool[...]

    arrived(pool.at[pl.ds(0, 7)], pool_out)
    arrived(got_coarse.at[pl.ds(0, 7)], coarse_out)

    def left(t, carry):
        for phase in range(6):
            rows = HALF if phase in (0, 5) else 3 * PIECE
            arrived(part.at[t, pl.ds(0, rows)], ar_out.at[phase, t])
        return carry

    lax.fori_loop(0, 9, left, 0)


def store_kernel(gf_ref, gc_ref, gw_ref, gf_out, gc_out, gw_out, sem):
    pairs = [(gw_ref.at[t], gw_out.at[t]) for t in range(9)]
    for n in range(8):
        some = pl.ds(n * (PIX // 8), PIX // 8)
        pairs.append((gf_ref.at[some], gf_out.at[some]))
    pairs.append((gc_ref, gc_out))
    copies = [pltpu.make_async_copy(*pair, sem.at[n]) for n, pair in enumerate(pairs)]
    for copy in copies:
        copy.start()
    for copy in copies:
        copy.wait()


def per_device(fine_input, coarse_feat, conv_weight, step_scale, timesteps, cotangent):
    anywhere = pl.BlockSpec(memory_space=pl.ANY)
    vmem = pl.BlockSpec(memory_space=pltpu.VMEM)
    buf = pltpu.VMEM
    dma = pltpu.SemaphoreType.DMA
    def in_hbm(array, shape):
        return pltpu.with_memory_space_constraint(array.reshape(shape), pltpu.HBM)

    results = pl.pallas_call(
        fused_kernel,
        name="fused",
        out_shape=(
            pltpu.VMEM((PIX, C), BF),
            pltpu.VMEM((C, C), BF),
            pltpu.VMEM((9, C, C), F32),
        ),
        in_specs=[pl.BlockSpec(memory_space=pltpu.SMEM)] + [anywhere] * 5,
        out_specs=(vmem, vmem, vmem),
        scratch_shapes=[
            buf((1000, C), F32),
            buf((ROWS, COLS, C), BF),
            buf((ROWS, COLS, C), BF),
            buf((9, C, C), BF),
            buf((3, 3 * C, C), BF),
            buf(((ROWS + 2) * COLS, 3 * C), BF),
            buf((C, PIX), BF),
            buf((PIX, C), F32),
            buf((2, ROWS, C), F32),
            buf((2, ROWS, C), BF),
            buf((2, ROWS, C), BF),
            buf((2, COLS, C), BF),
            buf((4, 16, C), BF),
            buf((8, 32, C), BF),
            buf((2, COLS, 128), F32),
            buf((2, ROWS, C), F32),
            buf((8, 32, C), BF),
            buf((C, C), BF),
            buf((9, C, C), BF),
            buf((9, HALF, C), BF),
            buf((9, HALF, C), BF),
            buf((9, 4, PIECE, C), BF),
            buf((9, 4, PIECE, C), BF),
            buf((9, 4, PIECE, C), BF),
            buf((9, C, C), BF),
            buf((2, COLS, 128), F32),
            dma((5,)),
            dma((8,)),
            dma((8,)),
            dma,
            dma((8,)),
            dma,
            dma,
            dma((6, 9)),
            dma((6, 9)),
        ],
        compiler_params=pltpu.CompilerParams(
            collective_id=0, has_side_effects=True, vmem_limit_bytes=40 * 2**20
        ),
        cost_estimate=pl.CostEstimate(
            flops=2 * 2 * 9 * PIX * C * C, bytes_accessed=12 * 2**20, transcendentals=PIX * C
        ),
    )(
        timesteps,
        in_hbm(step_scale, step_scale.shape),
        in_hbm(fine_input, (ROWS, COLS, C)),
        in_hbm(coarse_feat, (C, C)),
        in_hbm(conv_weight, (9, C, C)),
        in_hbm(cotangent, (ROWS, COLS, C)),
    )
    gf, gc, gw = pl.pallas_call(
        store_kernel,
        name="store",
        out_shape=(
            jax.ShapeDtypeStruct((PIX, C), BF),
            jax.ShapeDtypeStruct((C, C), BF),
            jax.ShapeDtypeStruct((9, C, C), F32),
        ),
        in_specs=[vmem] * 3,
        out_specs=(anywhere, anywhere, anywhere),
        scratch_shapes=[dma((18,))],
        compiler_params=pltpu.CompilerParams(vmem_limit_bytes=2**20),
    )(*(pltpu.with_memory_space_constraint(result, pltpu.VMEM) for result in results))
    return gf.reshape(1, ROWS, COLS, C), gc.reshape(1, 1, C, C), gw.reshape(3, 3, C, C)


def solution(mesh):
    return jax.shard_map(
        per_device,
        mesh=mesh,
        in_specs=(
            P(None, "row", "col", None),
            P(None, ("row", "col"), None, None),
            P(),
            P(),
            P(),
            P(None, "row", "col", None),
        ),
        out_specs=(P(None, "row", "col", None), P(None, ("row", "col"), None, None), P()),
        check_vma=False,
    )
```

time: 58.2 us -> 45.8 us (0.79)
  Pallas kernels: 51.2 us -> 44.4 us
  local copies, waits for them, and re-layouts: 5.48 us -> 0 us
    unnamed x10 -> x0, local copies, waits for them, and re-layouts: 5.48 us -> none
    pallas_call x1, Pallas kernels: 46.7 us -> 42.1 us  [per_device(): pl.pallas_call(fused_kernel, name='fused', out_shape=(pltpu.VMEM((PIX, C)...]
    pallas_call x1, Pallas kernels: 4.52 us -> 2.27 us  [per_device(): pl.pallas_call(store_kernel, name='store', out_shape=(jax.ShapeDtypeStruc...]
where the time goes in v2:
time: 45.8 us; the launch traced here: 45.6 us
  Pallas kernels  44.4 us (97%)
  between operations  1.29 us (3%)
    pallas_call x1, Pallas kernels, per_device(): pl.pallas_call(fused_kernel, name='fused', out_shape=(pltpu.VMEM((PIX, C)...  42.1 us
    pallas_call x1, Pallas kernels, per_device(): pl.pallas_call(store_kernel, name='store', out_shape=(jax.ShapeDtypeStruc...  2.27 us

profile of v2, /device:TPU:1, one launch (start us, length us, event | category | flops | bytes accessed | tf_op | source)
XLA Modules:
  0.0 45.6 jit_solution(13979920925371971128)
XLA Ops:
  1.3 42.1 %fused.1 = (bf16[4096,256]{1,0:T(8,128)(2,1)S(1)}, bf16[256,256]{1,0:T(8,128)(2,1)S(1)}, f32[9,256,256]{2,1,0:T(8,128)S(1)}) custom-call(s32[1]{0:T(128)S(6)} %copy.9.ts_ref, f32[1000,256]{1,0:T(8,128)} %ss_hbm.1, bf16[32,128,256]{2,1,0:T(8,128)(2,1)} %bitcast.8, bf16[256,256]{1,0:T(8,128)(2,1)} %bitcast.12, bf16[9,256,256]{2,1,0:T(8,128)(2,1)} %bitcast.11, ...), custom_call_target="tpu_custom_call" | custom-call | flops 9663676416 | bytes 12582912 | tf_op jit(solution)/shard_map/fused/pallas_call | solution.py:375
  43.4 2.3 %store.1 = (bf16[4096,256]{1,0:T(8,128)(2,1)}, bf16[256,256]{1,0:T(8,128)(2,1)}, f32[9,256,256]{2,1,0:T(8,128)}) custom-call(bf16[4096,256]{1,0:T(8,128)(2,1)S(1)} %get-tuple-element.9.gf_ref, bf16[256,256]{1,0:T(8,128)(2,1)S(1)} %get-tuple-element.10.gc_ref, f32[9,256,256]{2,1,0:T(8,128)S(1)} %get-tuple-element.11.gw_ref), custom_call_target="tpu_custom_call" | custom-call | tf_op jit(solution)/shard_map/store/pallas_call | solution.py:436

commit v3 on v2

--- a/solution.py
+++ b/solution.py
@@ -16,8 +16,7 @@
 GRID = (16, 8)
 STRIPS = 8
 PIECE = C // 8
-HALF = C // 2
-WHEN = ((1, 2, 3), (4, 6, 7), (8, 10, 11), (12, 13, 14), (15, 16, 17), (16, 17, 18))
+WHEN = ((2, 5, 7), (7, 10, 11), (11, 12, 13), (14, 15, 16))
 
 
 def place(x, y, z, k):
@@ -31,18 +30,17 @@
 
 
 def fused_kernel(
-    ts_ref, ss_hbm, fine_hbm, coarse_hbm, w_hbm, cot_hbm,
+    ts, ss_hbm, fine_hbm, coarse_hbm, w_hbm, cot_hbm,
     gf_ref, gc_ref, gw_ref,
-    ss, cot, fine, w, wcat, dcat, act_t, slope,
+    ss, cot, fine, coarse, w, wcat, dcat, act_t, slope,
     edge32, edge, got_edge, got_row, got_corner, got_coarse, up, patch,
-    pool, got_pool, part, pair, half_sum, stack1, stack2, stack3, whole, pooled_rows,
+    pool, got_pool, part, stack1, stack2, stack3, whole, pooled_rows,
     load_sem, out_sem, in_sem, coarse_out, coarse_in, pool_out, pool_in, ar_out, ar_in,
 ):
     row, col = lax.axis_index("row"), lax.axis_index("col")
     y, z_hi, k, z_lo, x = row // 4, (row // 2) % 2, row % 2, col // 4, col % 4
     z = z_hi * 2 + z_lo
     here = (x, y, z, k)
-    twin = place(x, y, z, 1 - k)
 
     down, upw, right, left = (row + 1) % 16, (row + 15) % 16, (col + 1) % 8, (col + 7) % 8
     partners = [(row, (col + d) % 8) for d in range(1, 8)]
@@ -50,33 +48,22 @@
     partners += [(a, b) for a in (down, upw) for b in (left, right)]
     partners += [other(1, d, 0, *here) for d in range(1, 4)]
     partners += [place(x, y, (z + 2) % 4, k), place(x, y, 3 - z, k)]
+    partners += [other(axis, d, 1, *here) for axis in range(3) for d in range(1, 4)]
     barrier = pltpu.get_barrier_semaphore()
     for partner in partners:
         pl.semaphore_signal(barrier, inc=1, device_id=partner, device_id_type=MESH)
 
     loads = [
-        pltpu.make_async_copy(cot_hbm, cot, load_sem.at[0]),
-        pltpu.make_async_copy(ss_hbm, ss, load_sem.at[1]),
-        pltpu.make_async_copy(w_hbm, w, load_sem.at[2]),
-        pltpu.make_async_copy(fine_hbm, fine, load_sem.at[3]),
-        pltpu.make_async_copy(
-            coarse_hbm.at[pl.ds(col * 32, 32)], got_coarse.at[col], load_sem.at[4]
-        ),
+        pltpu.make_async_copy(src, dst, load_sem.at[n])
+        for n, (src, dst) in enumerate(
+            (
+                (coarse_hbm, coarse), (cot_hbm, cot),
+                (ss_hbm, ss), (w_hbm, w), (fine_hbm, fine),
+            )
+        )
     ]
     for copy in loads:
         copy.start()
-
-    loads[0].wait()
-
-    def take_edge(r, carry):
-        edge32[0, pl.ds(r, 1), :] = cot[r, 0:16, :].astype(F32)[0:1]
-        edge32[1, pl.ds(r, 1), :] = cot[r, COLS - 16 : COLS, :].astype(F32)[15:16]
-        return carry
-
-    lax.fori_loop(0, ROWS, take_edge, 0, unroll=8)
-    edge[...] = edge32[...].astype(BF)
-
-    pl.semaphore_wait(barrier, len(partners))
 
     def push(src, dst, send, recv, to):
         copy = pltpu.make_async_remote_copy(
@@ -90,13 +77,30 @@
         m = n % 4
         return ((z_lo + n // 4) % 2) * 4 + (x + (m * (m + 1) // 2)) % 4
 
+    loads[0].wait()
+    pl.semaphore_wait(barrier, len(partners))
     for n in range(7, 0, -1):
         to = near_strip(n)
         push(
-            coarse_hbm.at[pl.ds(to * 32, 32)], got_coarse.at[col],
+            coarse.at[pl.ds(pl.multiple_of(to * 32, 32), 32)], got_coarse.at[col],
             coarse_out, coarse_in.at[col], (row, to),
         )
-    sent = []
+
+    loads[1].wait()
+
+    def take_edge(r, carry):
+        edge32[0, pl.ds(r, 1), :] = cot[r, 0:16, :].astype(F32)[0:1]
+        edge32[1, pl.ds(r, 1), :] = cot[r, COLS - 16 : COLS, :].astype(F32)[15:16]
+        return carry
+
+    lax.fori_loop(0, ROWS, take_edge, 0, unroll=8)
+    edge[...] = edge32[...].astype(BF)
+    sent = [
+        push(edge.at[1], got_edge.at[0], out_sem.at[0], in_sem.at[0], (row, right)),
+        push(edge.at[0], got_edge.at[1], out_sem.at[1], in_sem.at[1], (row, left)),
+    ]
+    sent.append(push(cot.at[ROWS - 1], got_row.at[0], out_sem.at[2], in_sem.at[2], (down, col)))
+    sent.append(push(cot.at[0], got_row.at[1], out_sem.at[3], in_sem.at[3], (upw, col)))
     for n, (src_row, first, to) in enumerate(
         (
             (ROWS - 1, COLS - 16, (down, right)),
@@ -107,17 +111,13 @@
     ):
         sent.append(
             push(
-                cot_hbm.at[src_row, pl.ds(first, 16)], got_corner.at[n],
-                out_sem.at[n], in_sem.at[n], to,
+                cot.at[src_row, pl.ds(first, 16)], got_corner.at[n],
+                out_sem.at[4 + n], in_sem.at[4 + n], to,
             )
         )
-    sent.append(push(cot_hbm.at[ROWS - 1], got_row.at[0], out_sem.at[4], in_sem.at[4], (down, col)))
-    sent.append(push(cot_hbm.at[0], got_row.at[1], out_sem.at[5], in_sem.at[5], (upw, col)))
-    sent.append(push(edge.at[1], got_edge.at[0], out_sem.at[6], in_sem.at[6], (row, right)))
-    sent.append(push(edge.at[0], got_edge.at[1], out_sem.at[7], in_sem.at[7], (row, left)))
-
-    loads[1].wait()
-    picked = ss[pl.ds(ts_ref[0], 1), :]
+
+    loads[2].wait()
+    picked = ss[pl.ds(ts[0], 1), :]
 
     def scaled(raw):
         return (raw.astype(F32) * picked).astype(BF)
@@ -133,7 +133,7 @@
 
     lax.fori_loop(0, ROWS, shift_row, 0, unroll=2)
 
-    loads[2].wait()
+    loads[3].wait()
 
     def turn_weight(i, carry):
         for j in range(3):
@@ -142,21 +142,24 @@
 
     lax.fori_loop(0, 3, turn_weight, 0)
 
-    loads[3].wait()
     loads[4].wait()
 
     def activate(n, carry):
         strip = near_strip(n)
 
+        @pl.when(n == 0)
+        def _():
+            got_coarse[strip] = coarse[pl.ds(pl.multiple_of(strip * 32, 32), 32), :]
+
         @pl.when(n > 0)
         def _():
             some = got_coarse.at[strip]
             pltpu.make_async_copy(some, some, coarse_in.at[strip]).wait()
 
-        coarse = got_coarse[strip].astype(F32)
+        cells = got_coarse[strip].astype(F32)
         for q in range(4):
             for half in range(2):
-                up[half, pl.ds(q, 32, stride=4), :] = coarse[:, half * 128 : half * 128 + 128]
+                up[half, pl.ds(q, 32, stride=4), :] = cells[:, half * 128 : half * 128 + 128]
 
         def fine_row(q, carry):
             r = strip * 4 + q
@@ -177,7 +180,7 @@
     keep_left = jnp.where(col > 0, 1.0, 0.0)
     keep_right = jnp.where(col < 7, 1.0, 0.0)
 
-    for copy in sent:
+    for copy in sent[:2]:
         copy.wait()
     patch[0] = scaled(got_edge[0]).astype(F32) * keep_left
     patch[1] = scaled(got_edge[1]).astype(F32) * keep_right
@@ -194,83 +197,80 @@
 
     lax.fori_loop(0, ROWS, patch_row, 0, unroll=4)
     spot_row = lax.broadcasted_iota(jnp.int32, (COLS, C), 0)
-    for n, (start, keep) in enumerate(((0, keep_top), ((ROWS + 1) * COLS, keep_bottom))):
-        wide = scaled(got_row[n]).astype(F32) * keep
-        near = scaled(got_corner[2 * n]).astype(F32)[15:16] * (keep * keep_left)
-        far = scaled(got_corner[2 * n + 1]).astype(F32)[0:1] * (keep * keep_right)
-        at = pl.ds(start, COLS)
-        dcat[at, C : 2 * C] = wide.astype(BF)
-        dcat[at, 2 * C : 3 * C] = jnp.where(spot_row == 0, near, pltpu.roll(wide, 1, 0)).astype(BF)
-        dcat[at, 0:C] = jnp.where(
-            spot_row == COLS - 1, far, pltpu.roll(wide, COLS - 1, 0)
-        ).astype(BF)
-
-    my_half = pl.ds(pl.multiple_of(k * HALF, HALF), HALF)
-    twin_half = pl.ds(pl.multiple_of((1 - k) * HALF, HALF), HALF)
-
-    def one_hot(axis):
-        return (1 - axis) * (2 - axis) // 2, axis * (2 - axis), axis * (axis - 1) // 2
+
+    def outer_rows():
+        for copy in sent[2:]:
+            copy.wait()
+        for n, (start, keep) in enumerate(((0, keep_top), ((ROWS + 1) * COLS, keep_bottom))):
+            wide = scaled(got_row[n]).astype(F32) * keep
+            near = scaled(got_corner[2 * n]).astype(F32)[15:16] * (keep * keep_left)
+            far = scaled(got_corner[2 * n + 1]).astype(F32)[0:1] * (keep * keep_right)
+            at = pl.ds(start, COLS)
+            dcat[at, C : 2 * C] = wide.astype(BF)
+            dcat[at, 2 * C : 3 * C] = jnp.where(
+                spot_row == 0, near, pltpu.roll(wide, 1, 0)
+            ).astype(BF)
+            dcat[at, 0:C] = jnp.where(
+                spot_row == COLS - 1, far, pltpu.roll(wide, COLS - 1, 0)
+            ).astype(BF)
 
     def mine(axis):
-        a, b, c = one_hot(axis)
-        return a * x + b * y + c * z
+        return here[axis] * 2 + k
+
+    def eight(axis):
+        return [
+            (((here[axis] + d) % 4) * 2 + (k + flip) % 2, other(axis, d, flip, *here))
+            for d, flip in ((2, 1), (2, 0), (1, 1), (3, 1), (1, 0), (3, 0), (0, 1))
+        ]
 
     def peers(axis):
-        a, b, c = one_hot(axis)
-        me = mine(axis)
-        for d in range(1, 4):
-            yield (me + d) % 4, place((x + d * a) % 4, (y + d * b) % 4, (z + d * c) % 4, k)
+        return [other(axis, d, 0, *here) for d in (2, 1, 3)]
 
     def arrived(some, sem):
         pltpu.make_async_copy(some, some, sem).wait()
 
     def total(stack, t):
         out = stack[t, 0].astype(F32)
-        for n in range(1, 4):
+        for n in range(1, stack.shape[1]):
             out = out + stack[t, n].astype(F32)
         return out.astype(BF)
 
     def quarter(m):
         return pl.ds(pl.multiple_of(m * PIECE, PIECE), PIECE)
 
-    def step0(t, j):
-        arrived(pair.at[t], ar_in.at[0, t])
-        half_sum[t] = (part[t, my_half, :].astype(F32) + pair[t].astype(F32)).astype(BF)
-        me = mine(j)
-        for m, to in peers(j):
-            push(half_sum.at[t, quarter(m)], stack1.at[t, me], ar_out.at[1, t], ar_in.at[1, t], to)
-        stack1[t, me] = half_sum[t, quarter(me), :]
+    def three(stack, first, rows):
+        return stack.at[pl.ds(first, 3), pl.ds(0, rows)]
 
     def exchange(before, after, phase):
-        def step(t, j):
-            arrived(before.at[t, pl.ds(0, 3)], ar_in.at[phase, t])
-            axis = (j + phase) % 3
-            me = mine(axis)
-            after[t, me] = total(before, t)
-            for _, to in peers(axis):
-                push(
-                    after.at[t, me], after.at[t, me],
-                    ar_out.at[phase + 1, t], ar_in.at[phase + 1, t], to,
-                )
+        def step(g, first):
+            arrived(three(before, first, before.shape[1] - 1), ar_in.at[phase - 1, g])
+            for j in range(3):
+                after[first + j, here[(j + phase) % 3]] = total(before, first + j)
+            for j in range(3):
+                t, axis = first + j, (j + phase) % 3
+                for to in peers(axis):
+                    push(
+                        after.at[t, here[axis]], after.at[t, here[axis]],
+                        ar_out.at[phase], ar_in.at[phase, g], to,
+                    )
 
         return step
 
-    def step3(t, j):
-        arrived(stack3.at[t, pl.ds(0, 3)], ar_in.at[3, t])
-        at = quarter(4 * k + mine(j))
-        whole[t, at, :] = total(stack3, t)
-        for _, to in peers(j):
-            push(whole.at[t, at], whole.at[t, at], ar_out.at[4, t], ar_in.at[4, t], to)
-
-    def step4(t, j):
-        arrived(whole.at[t, pl.ds(0, 3 * PIECE)], ar_in.at[4, t])
-        push(whole.at[t, my_half], whole.at[t, my_half], ar_out.at[5, t], ar_in.at[5, t], twin)
+    def step3(g, first):
+        arrived(three(stack3, first, 3), ar_in.at[2, g])
+        for j in range(3):
+            whole[first + j, quarter(mine(j)), :] = total(stack3, first + j)
+        for j in range(3):
+            some = whole.at[first + j, quarter(mine(j))]
+            for _, to in eight(j):
+                push(some, some, ar_out.at[3], ar_in.at[3, g], to)
 
     scale = 1.0 / math.sqrt(PIX * GRID[0] * GRID[1])
 
-    def step5(t, j):
-        arrived(whole.at[t, pl.ds(0, HALF)], ar_in.at[5, t])
-        gw_ref[t] = whole[t].astype(F32) * scale
+    def step4(g, first):
+        arrived(three(whole, first, 7 * PIECE), ar_in.at[3, g])
+        for j in range(3):
+            gw_ref[first + j] = whole[first + j].astype(F32) * scale
 
     def first_tap(g):
         return 3 * ((4 - g) % 3)
@@ -284,7 +284,9 @@
             ).astype(BF)
         for j in range(3):
             t = first + j
-            push(part.at[t, twin_half], pair.at[t], ar_out.at[0, t], ar_in.at[0, t], twin)
+            for m, to in eight(j):
+                push(part.at[t, quarter(m)], stack1.at[t, mine(j)], ar_out.at[0], ar_in.at[0, g], to)
+            stack1[t, mine(j)] = part[t, quarter(mine(j)), :]
 
     def strip(n):
         c = (col + 1 + n) % 8
@@ -315,9 +317,13 @@
         def _():
             got_pool[slot, :] = pool[n]
 
-    steps = (step0, exchange(stack1, stack2, 1), exchange(stack2, stack3, 2), step3, step4, step5)
+    steps = (exchange(stack1, stack2, 1), exchange(stack2, stack3, 2), step3, step4)
 
     def slot(u, carry):
+        @pl.when(u == 1)
+        def _():
+            outer_rows()
+
         @pl.when(u < 3)
         def _():
             taps(u)
@@ -330,7 +336,7 @@
             @pl.when((u == first) | (u == second) | (u == third))
             def _():
                 g = jnp.where(u == first, 0, jnp.where(u == second, 1, 2))
-                lax.fori_loop(0, 3, lambda j, c: (step(first_tap(g) + j, j), c)[1], 0)
+                step(g, first_tap(g))
 
         return carry
 
@@ -342,13 +348,8 @@
     arrived(pool.at[pl.ds(0, 7)], pool_out)
     arrived(got_coarse.at[pl.ds(0, 7)], coarse_out)
 
-    def left(t, carry):
-        for phase in range(6):
-            rows = HALF if phase in (0, 5) else 3 * PIECE
-            arrived(part.at[t, pl.ds(0, rows)], ar_out.at[phase, t])
-        return carry
-
-    lax.fori_loop(0, 9, left, 0)
+    for phase, count in enumerate((7, 3, 3, 7)):
+        arrived(dcat.at[pl.ds(0, 9 * count * PIECE // 3)], ar_out.at[phase])
 
 
 def store_kernel(gf_ref, gc_ref, gw_ref, gf_out, gc_out, gw_out, sem):
@@ -386,6 +387,7 @@
             buf((1000, C), F32),
             buf((ROWS, COLS, C), BF),
             buf((ROWS, COLS, C), BF),
+            buf((C, C), BF),
             buf((9, C, C), BF),
             buf((3, 3 * C, C), BF),
             buf(((ROWS + 2) * COLS, 3 * C), BF),
@@ -402,9 +404,7 @@
             buf((8, 32, C), BF),
             buf((C, C), BF),
             buf((9, C, C), BF),
-            buf((9, HALF, C), BF),
-            buf((9, HALF, C), BF),
-            buf((9, 4, PIECE, C), BF),
+            buf((9, 8, PIECE, C), BF),
             buf((9, 4, PIECE, C), BF),
             buf((9, 4, PIECE, C), BF),
             buf((9, C, C), BF),
@@ -416,8 +416,8 @@
             dma((8,)),
             dma,
             dma,
-            dma((6, 9)),
-            dma((6, 9)),
+            dma((4,)),
+            dma((4, 3)),
         ],
         compiler_params=pltpu.CompilerParams(
             collective_id=0, has_side_effects=True, vmem_limit_bytes=40 * 2**20

time: 45.8 us -> 42.2 us (0.921)
  Pallas kernels: 44.4 us -> 40.8 us
    pallas_call x1, Pallas kernels: 42.1 us -> 38.5 us  [per_device(): pl.pallas_call(fused_kernel, name='fused', out_shape=(pltpu.VMEM((PIX, C)...]
where the time goes in v3:
time: 42.2 us; the launch traced here: 42.1 us
  Pallas kernels  40.8 us (97%)
  between operations  1.29 us (3%)
    pallas_call x1, Pallas kernels, per_device(): pl.pallas_call(fused_kernel, name='fused', out_shape=(pltpu.VMEM((PIX, C)...  38.5 us
    pallas_call x1, Pallas kernels, per_device(): pl.pallas_call(store_kernel, name='store', out_shape=(jax.ShapeDtypeStruc...  2.27 us

profile of v3, /device:TPU:1, one launch (start us, length us, event | category | flops | bytes accessed | tf_op | source)
XLA Modules:
  0.0 42.1 jit_solution(8597716456148956571)
XLA Ops:
  1.3 38.5 %fused.1 = (bf16[4096,256]{1,0:T(8,128)(2,1)S(1)}, bf16[256,256]{1,0:T(8,128)(2,1)S(1)}, f32[9,256,256]{2,1,0:T(8,128)S(1)}) custom-call(s32[1]{0:T(128)S(6)} %copy.9.ts, f32[1000,256]{1,0:T(8,128)} %ss_hbm.1, bf16[32,128,256]{2,1,0:T(8,128)(2,1)} %bitcast.8, bf16[256,256]{1,0:T(8,128)(2,1)} %bitcast.12, bf16[9,256,256]{2,1,0:T(8,128)(2,1)} %bitcast.11, ...), custom_call_target="tpu_custom_call" | custom-call | flops 9663676416 | bytes 12582912 | tf_op jit(solution)/shard_map/fused/pallas_call | solution.py:376
  39.8 2.3 %store.1 = (bf16[4096,256]{1,0:T(8,128)(2,1)}, bf16[256,256]{1,0:T(8,128)(2,1)}, f32[9,256,256]{2,1,0:T(8,128)}) custom-call(bf16[4096,256]{1,0:T(8,128)(2,1)S(1)} %get-tuple-element.9.gf_ref, bf16[256,256]{1,0:T(8,128)(2,1)S(1)} %get-tuple-element.10.gc_ref, f32[9,256,256]{2,1,0:T(8,128)S(1)} %get-tuple-element.11.gw_ref), custom_call_target="tpu_custom_call" | custom-call | tf_op jit(solution)/shard_map/store/pallas_call | solution.py:436

commit v4 on v3

--- a/solution.py
+++ b/solution.py
@@ -11,12 +11,13 @@
 MESH = pl.DeviceIdType.MESH
 BF = jnp.bfloat16
 F32 = jnp.float32
+TN = (((0,), (0,)), ((), ()))
 ROWS, COLS, C = 32, 128, 256
 PIX = ROWS * COLS
 GRID = (16, 8)
 STRIPS = 8
 PIECE = C // 8
-WHEN = ((2, 5, 7), (7, 10, 11), (11, 12, 13), (14, 15, 16))
+WHEN = ((2, 4, 6), (6, 8, 9), (10, 11, 12), (14, 15, 16))
 
 
 def place(x, y, z, k):
@@ -32,7 +33,7 @@
 def fused_kernel(
     ts, ss_hbm, fine_hbm, coarse_hbm, w_hbm, cot_hbm,
     gf_ref, gc_ref, gw_ref,
-    ss, cot, fine, coarse, w, wcat, dcat, act_t, slope,
+    ss, cot, fine, coarse, w, wcat, dcat, act, slope,
     edge32, edge, got_edge, got_row, got_corner, got_coarse, up, patch,
     pool, got_pool, part, stack1, stack2, stack3, whole, pooled_rows,
     load_sem, out_sem, in_sem, coarse_out, coarse_in, pool_out, pool_in, ar_out, ar_in,
@@ -167,7 +168,7 @@
             sig = 0.5 * jnp.tanh(0.5 * hidden) + 0.5
             value = hidden * sig
             at = pl.ds(pl.multiple_of(r * COLS, COLS), COLS)
-            act_t[:, at] = value.astype(BF).T
+            act[at, :] = value.astype(BF)
             slope[at, :] = sig + value * (1.0 - sig)
             return carry
 
@@ -278,10 +279,9 @@
     def taps(g):
         first = first_tap(g)
         at = pl.ds(pl.multiple_of(2 * COLS - first // 3 * COLS, COLS), PIX)
-        for j in range(3):
-            part[first + j] = jnp.dot(
-                act_t[...], dcat[at, j * C : (j + 1) * C], preferred_element_type=F32
-            ).astype(BF)
+        row_of_taps = lax.dot_general(act[...], dcat[at, :], TN, preferred_element_type=F32)
+        for j in range(3):
+            part[first + j] = row_of_taps[:, j * C : (j + 1) * C].astype(BF)
         for j in range(3):
             t = first + j
             for m, to in eight(j):
@@ -391,7 +391,7 @@
             buf((9, C, C), BF),
             buf((3, 3 * C, C), BF),
             buf(((ROWS + 2) * COLS, 3 * C), BF),
-            buf((C, PIX), BF),
+            buf((PIX, C), BF),
             buf((PIX, C), F32),
             buf((2, ROWS, C), F32),
             buf((2, ROWS, C), BF),

time: 42.2 us -> 40.8 us (0.967)
  Pallas kernels: 40.8 us -> 39.4 us
    pallas_call x1, Pallas kernels: 38.5 us -> 37.1 us  [per_device(): pl.pallas_call(fused_kernel, name='fused', out_shape=(pltpu.VMEM((PIX, C)...]
where the time goes in v4:
time: 40.8 us; the launch traced here: 40.7 us
  Pallas kernels  39.4 us (97%)
  between operations  1.29 us (3%)
    pallas_call x1, Pallas kernels, per_device(): pl.pallas_call(fused_kernel, name='fused', out_shape=(pltpu.VMEM((PIX, C)...  37.1 us
    pallas_call x1, Pallas kernels, per_device(): pl.pallas_call(store_kernel, name='store', out_shape=(jax.ShapeDtypeStruc...  2.27 us

profile of v4, /device:TPU:1, one launch (start us, length us, event | category | flops | bytes accessed | tf_op | source)
XLA Modules:
  0.0 40.7 jit_solution(12502680144983695283)
XLA Ops:
  1.3 37.1 %fused.1 = (bf16[4096,256]{1,0:T(8,128)(2,1)S(1)}, bf16[256,256]{1,0:T(8,128)(2,1)S(1)}, f32[9,256,256]{2,1,0:T(8,128)S(1)}) custom-call(s32[1]{0:T(128)S(6)} %copy.9.ts, f32[1000,256]{1,0:T(8,128)} %ss_hbm.1, bf16[32,128,256]{2,1,0:T(8,128)(2,1)} %bitcast.8, bf16[256,256]{1,0:T(8,128)(2,1)} %bitcast.12, bf16[9,256,256]{2,1,0:T(8,128)(2,1)} %bitcast.11, ...), custom_call_target="tpu_custom_call" | custom-call | flops 9663676416 | bytes 12582912 | tf_op jit(solution)/shard_map/fused/pallas_call | solution.py:376
  38.4 2.3 %store.1 = (bf16[4096,256]{1,0:T(8,128)(2,1)}, bf16[256,256]{1,0:T(8,128)(2,1)}, f32[9,256,256]{2,1,0:T(8,128)}) custom-call(bf16[4096,256]{1,0:T(8,128)(2,1)S(1)} %get-tuple-element.9.gf_ref, bf16[256,256]{1,0:T(8,128)(2,1)S(1)} %get-tuple-element.10.gc_ref, f32[9,256,256]{2,1,0:T(8,128)S(1)} %get-tuple-element.11.gw_ref), custom_call_target="tpu_custom_call" | custom-call | tf_op jit(solution)/shard_map/store/pallas_call | solution.py:436

commit v5 on v4

--- a/solution.py
+++ b/solution.py
@@ -17,7 +17,7 @@
 GRID = (16, 8)
 STRIPS = 8
 PIECE = C // 8
-WHEN = ((2, 4, 6), (6, 8, 9), (10, 11, 12), (14, 15, 16))
+WHEN = ((3, 4, 5), (6, 7, 8), (8, 9, 11), (12, 13, 14))
 
 
 def place(x, y, z, k):
@@ -34,7 +34,7 @@
     ts, ss_hbm, fine_hbm, coarse_hbm, w_hbm, cot_hbm,
     gf_ref, gc_ref, gw_ref,
     ss, cot, fine, coarse, w, wcat, dcat, act, slope,
-    edge32, edge, got_edge, got_row, got_corner, got_coarse, up, patch,
+    rim, edge32, edge, got_edge, got_row, got_corner, got_coarse, up, patch,
     pool, got_pool, part, stack1, stack2, stack3, whole, pooled_rows,
     load_sem, out_sem, in_sem, coarse_out, coarse_in, pool_out, pool_in, ar_out, ar_in,
 ):
@@ -58,12 +58,13 @@
         pltpu.make_async_copy(src, dst, load_sem.at[n])
         for n, (src, dst) in enumerate(
             (
-                (coarse_hbm, coarse), (cot_hbm, cot),
+                (coarse_hbm, coarse), (cot_hbm.at[:, pl.ds(0, 16)], rim.at[0]),
+                (cot_hbm.at[:, pl.ds(COLS - 16, 16)], rim.at[1]), (cot_hbm, cot),
                 (ss_hbm, ss), (w_hbm, w), (fine_hbm, fine),
             )
         )
     ]
-    for copy in loads:
+    for copy in loads[:4]:
         copy.start()
 
     def push(src, dst, send, recv, to):
@@ -87,19 +88,24 @@
             coarse_out, coarse_in.at[col], (row, to),
         )
 
+    for copy in loads[4:]:
+        copy.start()
+
     loads[1].wait()
+    loads[2].wait()
 
     def take_edge(r, carry):
-        edge32[0, pl.ds(r, 1), :] = cot[r, 0:16, :].astype(F32)[0:1]
-        edge32[1, pl.ds(r, 1), :] = cot[r, COLS - 16 : COLS, :].astype(F32)[15:16]
+        edge32[0, pl.ds(r, 1), :] = rim[0, r].astype(F32)[0:1]
+        edge32[1, pl.ds(r, 1), :] = rim[1, r].astype(F32)[15:16]
         return carry
 
-    lax.fori_loop(0, ROWS, take_edge, 0, unroll=8)
+    lax.fori_loop(0, ROWS, take_edge, 0)
     edge[...] = edge32[...].astype(BF)
     sent = [
         push(edge.at[1], got_edge.at[0], out_sem.at[0], in_sem.at[0], (row, right)),
         push(edge.at[0], got_edge.at[1], out_sem.at[1], in_sem.at[1], (row, left)),
     ]
+    loads[3].wait()
     sent.append(push(cot.at[ROWS - 1], got_row.at[0], out_sem.at[2], in_sem.at[2], (down, col)))
     sent.append(push(cot.at[0], got_row.at[1], out_sem.at[3], in_sem.at[3], (upw, col)))
     for n, (src_row, first, to) in enumerate(
@@ -117,7 +123,7 @@
             )
         )
 
-    loads[2].wait()
+    loads[4].wait()
     picked = ss[pl.ds(ts[0], 1), :]
 
     def scaled(raw):
@@ -132,9 +138,9 @@
         dcat[at, 0:C] = pltpu.roll(wide, COLS - 1, 0).astype(BF)
         return carry
 
-    lax.fori_loop(0, ROWS, shift_row, 0, unroll=2)
-
-    loads[3].wait()
+    lax.fori_loop(0, ROWS, shift_row, 0)
+
+    loads[5].wait()
 
     def turn_weight(i, carry):
         for j in range(3):
@@ -143,7 +149,7 @@
 
     lax.fori_loop(0, 3, turn_weight, 0)
 
-    loads[4].wait()
+    loads[6].wait()
 
     def activate(n, carry):
         strip = near_strip(n)
@@ -172,7 +178,7 @@
             slope[at, :] = sig + value * (1.0 - sig)
             return carry
 
-        return lax.fori_loop(0, 4, fine_row, carry, unroll=2)
+        return lax.fori_loop(0, 4, fine_row, carry)
 
     lax.fori_loop(0, STRIPS, activate, 0)
 
@@ -196,7 +202,7 @@
         dcat[last, 0:C] = jnp.where(spot == 15, patch[1, pl.ds(r, 1), :], hi).astype(BF)
         return carry
 
-    lax.fori_loop(0, ROWS, patch_row, 0, unroll=4)
+    lax.fori_loop(0, ROWS, patch_row, 0)
     spot_row = lax.broadcasted_iota(jnp.int32, (COLS, C), 0)
 
     def outer_rows():
@@ -247,12 +253,12 @@
             arrived(three(before, first, before.shape[1] - 1), ar_in.at[phase - 1, g])
             for j in range(3):
                 after[first + j, here[(j + phase) % 3]] = total(before, first + j)
-            for j in range(3):
-                t, axis = first + j, (j + phase) % 3
-                for to in peers(axis):
+            for n in range(3):
+                for j in range(3):
+                    t, axis = first + j, (j + phase) % 3
                     push(
                         after.at[t, here[axis]], after.at[t, here[axis]],
-                        ar_out.at[phase], ar_in.at[phase, g], to,
+                        ar_out.at[phase], ar_in.at[phase, g], peers(axis)[n],
                     )
 
         return step
@@ -261,10 +267,10 @@
         arrived(three(stack3, first, 3), ar_in.at[2, g])
         for j in range(3):
             whole[first + j, quarter(mine(j)), :] = total(stack3, first + j)
-        for j in range(3):
-            some = whole.at[first + j, quarter(mine(j))]
-            for _, to in eight(j):
-                push(some, some, ar_out.at[3], ar_in.at[3, g], to)
+        for n in range(7):
+            for j in range(3):
+                some = whole.at[first + j, quarter(mine(j))]
+                push(some, some, ar_out.at[3], ar_in.at[3, g], eight(j)[n][1])
 
     scale = 1.0 / math.sqrt(PIX * GRID[0] * GRID[1])
 
@@ -282,11 +288,13 @@
         row_of_taps = lax.dot_general(act[...], dcat[at, :], TN, preferred_element_type=F32)
         for j in range(3):
             part[first + j] = row_of_taps[:, j * C : (j + 1) * C].astype(BF)
+        for n in range(7):
+            for j in range(3):
+                t = first + j
+                m, to = eight(j)[n]
+                push(part.at[t, quarter(m)], stack1.at[t, mine(j)], ar_out.at[0], ar_in.at[0, g], to)
         for j in range(3):
-            t = first + j
-            for m, to in eight(j):
-                push(part.at[t, quarter(m)], stack1.at[t, mine(j)], ar_out.at[0], ar_in.at[0, g], to)
-            stack1[t, mine(j)] = part[t, quarter(mine(j)), :]
+            stack1[first + j, mine(j)] = part[first + j, quarter(mine(j)), :]
 
     def strip(n):
         c = (col + 1 + n) % 8
@@ -340,16 +348,15 @@
 
         return carry
 
-    lax.fori_loop(0, WHEN[-1][-1] + 1, slot, 0)
+    lax.fori_loop(0, WHEN[-1][-1], slot, 0)
 
     arrived(got_pool.at[pl.ds(0, 7 * 32)], pool_in)
     gc_ref[...] = got_pool[...]
-
     arrived(pool.at[pl.ds(0, 7)], pool_out)
     arrived(got_coarse.at[pl.ds(0, 7)], coarse_out)
-
     for phase, count in enumerate((7, 3, 3, 7)):
         arrived(dcat.at[pl.ds(0, 9 * count * PIECE // 3)], ar_out.at[phase])
+    steps[-1](2, first_tap(2))
 
 
 def store_kernel(gf_ref, gc_ref, gw_ref, gf_out, gc_out, gw_out, sem):
@@ -393,6 +400,7 @@
             buf(((ROWS + 2) * COLS, 3 * C), BF),
             buf((PIX, C), BF),
             buf((PIX, C), F32),
+            buf((2, ROWS, 16, C), BF),
             buf((2, ROWS, C), F32),
             buf((2, ROWS, C), BF),
             buf((2, ROWS, C), BF),
@@ -409,7 +417,7 @@
             buf((9, 4, PIECE, C), BF),
             buf((9, C, C), BF),
             buf((2, COLS, 128), F32),
-            dma((5,)),
+            dma((7,)),
             dma((8,)),
             dma((8,)),
             dma,

time: 40.8 us -> 40.6 us (level)
  no operation moved by 1% of the time
where the time goes in v5:
time: 40.6 us; the launch traced here: 40.5 us
  Pallas kernels  39.2 us (97%)
  between operations  1.29 us (3%)
    pallas_call x1, Pallas kernels, per_device(): pl.pallas_call(fused_kernel, name='fused', out_shape=(pltpu.VMEM((PIX, C)...  36.9 us
    pallas_call x1, Pallas kernels, per_device(): pl.pallas_call(store_kernel, name='store', out_shape=(jax.ShapeDtypeStruc...  2.27 us

profile of v5, /device:TPU:1, one launch (start us, length us, event | category | flops | bytes accessed | tf_op | source)
XLA Modules:
  0.0 40.5 jit_solution(15244939806206138712)
XLA Ops:
  1.3 36.9 %fused.1 = (bf16[4096,256]{1,0:T(8,128)(2,1)S(1)}, bf16[256,256]{1,0:T(8,128)(2,1)S(1)}, f32[9,256,256]{2,1,0:T(8,128)S(1)}) custom-call(s32[1]{0:T(128)S(6)} %copy.9.ts, f32[1000,256]{1,0:T(8,128)} %ss_hbm.1, bf16[32,128,256]{2,1,0:T(8,128)(2,1)} %bitcast.8, bf16[256,256]{1,0:T(8,128)(2,1)} %bitcast.12, bf16[9,256,256]{2,1,0:T(8,128)(2,1)} %bitcast.11, ...), custom_call_target="tpu_custom_call" | custom-call | flops 9663676416 | bytes 12582912 | tf_op jit(solution)/shard_map/fused/pallas_call | solution.py:383
  38.2 2.3 %store.1 = (bf16[4096,256]{1,0:T(8,128)(2,1)}, bf16[256,256]{1,0:T(8,128)(2,1)}, f32[9,256,256]{2,1,0:T(8,128)}) custom-call(bf16[4096,256]{1,0:T(8,128)(2,1)S(1)} %get-tuple-element.9.gf_ref, bf16[256,256]{1,0:T(8,128)(2,1)S(1)} %get-tuple-element.10.gc_ref, f32[9,256,256]{2,1,0:T(8,128)S(1)} %get-tuple-element.11.gw_ref), custom_call_target="tpu_custom_call" | custom-call | tf_op jit(solution)/shard_map/store/pallas_call | solution.py:444

commit v6 on v5

--- a/solution.py
+++ b/solution.py
@@ -94,6 +94,25 @@
     loads[1].wait()
     loads[2].wait()
 
+    outer = []
+    for n, (side, src_row, to) in enumerate(
+        (
+            (1, ROWS - 1, (down, right)),
+            (0, ROWS - 1, (down, left)),
+            (1, 0, (upw, right)),
+            (0, 0, (upw, left)),
+        )
+    ):
+        outer.append(
+            push(
+                rim.at[side, src_row], got_corner.at[n],
+                out_sem.at[4 + n], in_sem.at[4 + n], to,
+            )
+        )
+
+    outer.append(push(cot_hbm.at[ROWS - 1], got_row.at[0], out_sem.at[2], in_sem.at[2], (down, col)))
+    outer.append(push(cot_hbm.at[0], got_row.at[1], out_sem.at[3], in_sem.at[3], (upw, col)))
+
     def take_edge(r, carry):
         edge32[0, pl.ds(r, 1), :] = rim[0, r].astype(F32)[0:1]
         edge32[1, pl.ds(r, 1), :] = rim[1, r].astype(F32)[15:16]
@@ -106,22 +125,6 @@
         push(edge.at[0], got_edge.at[1], out_sem.at[1], in_sem.at[1], (row, left)),
     ]
     loads[3].wait()
-    sent.append(push(cot.at[ROWS - 1], got_row.at[0], out_sem.at[2], in_sem.at[2], (down, col)))
-    sent.append(push(cot.at[0], got_row.at[1], out_sem.at[3], in_sem.at[3], (upw, col)))
-    for n, (src_row, first, to) in enumerate(
-        (
-            (ROWS - 1, COLS - 16, (down, right)),
-            (ROWS - 1, 0, (down, left)),
-            (0, COLS - 16, (upw, right)),
-            (0, 0, (upw, left)),
-        )
-    ):
-        sent.append(
-            push(
-                cot.at[src_row, pl.ds(first, 16)], got_corner.at[n],
-                out_sem.at[4 + n], in_sem.at[4 + n], to,
-            )
-        )
 
     loads[4].wait()
     picked = ss[pl.ds(ts[0], 1), :]
@@ -170,7 +173,9 @@
 
         def fine_row(q, carry):
             r = strip * 4 + q
-            hidden = fine[r].astype(F32) + jnp.concatenate([up[0], up[1]], axis=1)
+            hidden = fine[r].astype(F32) + jnp.concatenate(
+                [up[0, 0:COLS], up[1, 0:COLS]], axis=1
+            )
             sig = 0.5 * jnp.tanh(0.5 * hidden) + 0.5
             value = hidden * sig
             at = pl.ds(pl.multiple_of(r * COLS, COLS), COLS)
@@ -187,8 +192,8 @@
     keep_left = jnp.where(col > 0, 1.0, 0.0)
     keep_right = jnp.where(col < 7, 1.0, 0.0)
 
-    for copy in sent[:2]:
-        copy.wait()
+    for copy in sent:
+        copy.wait_recv()
     patch[0] = scaled(got_edge[0]).astype(F32) * keep_left
     patch[1] = scaled(got_edge[1]).astype(F32) * keep_right
     spot = lax.broadcasted_iota(jnp.int32, (16, C), 0)
@@ -206,8 +211,8 @@
     spot_row = lax.broadcasted_iota(jnp.int32, (COLS, C), 0)
 
     def outer_rows():
-        for copy in sent[2:]:
-            copy.wait()
+        for copy in outer:
+            copy.wait_recv()
         for n, (start, keep) in enumerate(((0, keep_top), ((ROWS + 1) * COLS, keep_bottom))):
             wide = scaled(got_row[n]).astype(F32) * keep
             near = scaled(got_corner[2 * n]).astype(F32)[15:16] * (keep * keep_left)
@@ -310,7 +315,7 @@
         tall = dh[0:COLS] + dh[COLS : 2 * COLS] + dh[2 * COLS : 3 * COLS] + dh[3 * COLS :]
         for half in range(2):
             lanes = slice(half * 128, half * 128 + 128)
-            pooled_rows[half] = tall[:, lanes]
+            pooled_rows[half, 0:COLS] = tall[:, lanes]
             cells = pooled_rows[half, pl.ds(0, 32, stride=4), :]
             for q in range(1, 4):
                 cells = cells + pooled_rows[half, pl.ds(q, 32, stride=4), :]
@@ -353,6 +358,8 @@
     arrived(got_pool.at[pl.ds(0, 7 * 32)], pool_in)
     gc_ref[...] = got_pool[...]
     arrived(pool.at[pl.ds(0, 7)], pool_out)
+    for copy in sent + outer:
+        copy.wait_send()
     arrived(got_coarse.at[pl.ds(0, 7)], coarse_out)
     for phase, count in enumerate((7, 3, 3, 7)):
         arrived(dcat.at[pl.ds(0, 9 * count * PIECE // 3)], ar_out.at[phase])
@@ -407,7 +414,7 @@
             buf((2, COLS, C), BF),
             buf((4, 16, C), BF),
             buf((8, 32, C), BF),
-            buf((2, COLS, 128), F32),
+            buf((2, COLS + 8, 128), F32),
             buf((2, ROWS, C), F32),
             buf((8, 32, C), BF),
             buf((C, C), BF),
@@ -416,7 +423,7 @@
             buf((9, 4, PIECE, C), BF),
             buf((9, 4, PIECE, C), BF),
             buf((9, C, C), BF),
-            buf((2, COLS, 128), F32),
+            buf((2, COLS + 8, 128), F32),
             dma((7,)),
             dma((8,)),
             dma((8,)),

time: 40.6 us -> 40.6 us (level)
  no operation moved by 1% of the time
where the time goes in v6:
time: 40.6 us; the launch traced here: 40.5 us
  Pallas kernels  39.2 us (97%)
  between operations  1.29 us (3%)
    pallas_call x1, Pallas kernels, per_device(): pl.pallas_call(fused_kernel, name='fused', out_shape=(pltpu.VMEM((PIX, C)...  36.9 us
    pallas_call x1, Pallas kernels, per_device(): pl.pallas_call(store_kernel, name='store', out_shape=(jax.ShapeDtypeStruc...  2.27 us

profile of v6, /device:TPU:1, one launch (start us, length us, event | category | flops | bytes accessed | tf_op | source)
XLA Modules:
  0.0 40.5 jit_solution(14338409222239759427)
XLA Ops:
  1.3 36.9 %fused.1 = (bf16[4096,256]{1,0:T(8,128)(2,1)S(1)}, bf16[256,256]{1,0:T(8,128)(2,1)S(1)}, f32[9,256,256]{2,1,0:T(8,128)S(1)}) custom-call(s32[1]{0:T(128)S(6)} %copy.9.ts, f32[1000,256]{1,0:T(8,128)} %ss_hbm.1, bf16[32,128,256]{2,1,0:T(8,128)(2,1)} %bitcast.8, bf16[256,256]{1,0:T(8,128)(2,1)} %bitcast.12, bf16[9,256,256]{2,1,0:T(8,128)(2,1)} %bitcast.11, ...), custom_call_target="tpu_custom_call" | custom-call | flops 9663676416 | bytes 12582912 | tf_op jit(solution)/shard_map/fused/pallas_call | solution.py:390
  38.2 2.3 %store.1 = (bf16[4096,256]{1,0:T(8,128)(2,1)}, bf16[256,256]{1,0:T(8,128)(2,1)}, f32[9,256,256]{2,1,0:T(8,128)}) custom-call(bf16[4096,256]{1,0:T(8,128)(2,1)S(1)} %get-tuple-element.9.gf_ref, bf16[256,256]{1,0:T(8,128)(2,1)S(1)} %get-tuple-element.10.gc_ref, f32[9,256,256]{2,1,0:T(8,128)S(1)} %get-tuple-element.11.gw_ref), custom_call_target="tpu_custom_call" | custom-call | tf_op jit(solution)/shard_map/store/pallas_call | solution.py:451

commit v7 on v6

--- a/solution.py
+++ b/solution.py
@@ -33,7 +33,7 @@
 def fused_kernel(
     ts, ss_hbm, fine_hbm, coarse_hbm, w_hbm, cot_hbm,
     gf_ref, gc_ref, gw_ref,
-    ss, cot, fine, coarse, w, wcat, dcat, act, slope,
+    ss, cot, fine, coarse, w, wcat, dcat, act,
     rim, edge32, edge, got_edge, got_row, got_corner, got_coarse, up, patch,
     pool, got_pool, part, stack1, stack2, stack3, whole, pooled_rows,
     load_sem, out_sem, in_sem, coarse_out, coarse_in, pool_out, pool_in, ar_out, ar_in,
@@ -180,7 +180,6 @@
             value = hidden * sig
             at = pl.ds(pl.multiple_of(r * COLS, COLS), COLS)
             act[at, :] = value.astype(BF)
-            slope[at, :] = sig + value * (1.0 - sig)
             return carry
 
         return lax.fori_loop(0, 4, fine_row, carry)
@@ -310,7 +309,17 @@
             term = jnp.dot(dcat[at, :], wcat[i], preferred_element_type=F32)
             acc = term if acc is None else acc + term
         at = pl.ds(pl.multiple_of(base, COLS), 4 * COLS)
-        dh = acc * slope[at, :]
+        cells = got_coarse[c].astype(F32)
+        for q in range(4):
+            for half in range(2):
+                up[half, pl.ds(q, 32, stride=4), :] = cells[:, half * 128 : half * 128 + 128]
+        upper = jnp.concatenate([up[0, 0:COLS], up[1, 0:COLS]], axis=1)
+        slopes = []
+        for q in range(4):
+            hidden = fine[c * 4 + q].astype(F32) + upper
+            sig = 0.5 * jnp.tanh(0.5 * hidden) + 0.5
+            slopes.append(sig + hidden * sig * (1.0 - sig))
+        dh = acc * jnp.concatenate(slopes, axis=0)
         gf_ref[at, :] = dh.astype(BF)
         tall = dh[0:COLS] + dh[COLS : 2 * COLS] + dh[2 * COLS : 3 * COLS] + dh[3 * COLS :]
         for half in range(2):
@@ -368,8 +377,8 @@
 
 def store_kernel(gf_ref, gc_ref, gw_ref, gf_out, gc_out, gw_out, sem):
     pairs = [(gw_ref.at[t], gw_out.at[t]) for t in range(9)]
-    for n in range(8):
-        some = pl.ds(n * (PIX // 8), PIX // 8)
+    for n in range(4):
+        some = pl.ds(n * (PIX // 4), PIX // 4)
         pairs.append((gf_ref.at[some], gf_out.at[some]))
     pairs.append((gc_ref, gc_out))
     copies = [pltpu.make_async_copy(*pair, sem.at[n]) for n, pair in enumerate(pairs)]
@@ -406,7 +415,6 @@
             buf((3, 3 * C, C), BF),
             buf(((ROWS + 2) * COLS, 3 * C), BF),
             buf((PIX, C), BF),
-            buf((PIX, C), F32),
             buf((2, ROWS, 16, C), BF),
             buf((2, ROWS, C), F32),
             buf((2, ROWS, C), BF),
@@ -458,7 +466,7 @@
         ),
         in_specs=[vmem] * 3,
         out_specs=(anywhere, anywhere, anywhere),
-        scratch_shapes=[dma((18,))],
+        scratch_shapes=[dma((14,))],
         compiler_params=pltpu.CompilerParams(vmem_limit_bytes=2**20),
     )(*(pltpu.with_memory_space_constraint(result, pltpu.VMEM) for result in results))
     return gf.reshape(1, ROWS, COLS, C), gc.reshape(1, 1, C, C), gw.reshape(3, 3, C, C)

time: 40.6 us -> 40.5 us (level)
  no operation moved by 1% of the time
where the time goes in v7:
time: 40.5 us; the launch traced here: 40.4 us
  Pallas kernels  39.1 us (97%)
  between operations  1.29 us (3%)
    pallas_call x1, Pallas kernels, per_device(): pl.pallas_call(fused_kernel, name='fused', out_shape=(pltpu.VMEM((PIX, C)...  36.8 us
    pallas_call x1, Pallas kernels, per_device(): pl.pallas_call(store_kernel, name='store', out_shape=(jax.ShapeDtypeStruc...  2.24 us

profile of v7, /device:TPU:1, one launch (start us, length us, event | category | flops | bytes accessed | tf_op | source)
XLA Modules:
  0.0 40.4 jit_solution(14443367803595100312)
XLA Ops:
  1.3 36.8 %fused.1 = (bf16[4096,256]{1,0:T(8,128)(2,1)S(1)}, bf16[256,256]{1,0:T(8,128)(2,1)S(1)}, f32[9,256,256]{2,1,0:T(8,128)S(1)}) custom-call(s32[1]{0:T(128)S(6)} %copy.9.ts, f32[1000,256]{1,0:T(8,128)} %ss_hbm.1, bf16[32,128,256]{2,1,0:T(8,128)(2,1)} %bitcast.8, bf16[256,256]{1,0:T(8,128)(2,1)} %bitcast.12, bf16[9,256,256]{2,1,0:T(8,128)(2,1)} %bitcast.11, ...), custom_call_target="tpu_custom_call" | custom-call | flops 9663676416 | bytes 12582912 | tf_op jit(solution)/shard_map/fused/pallas_call | solution.py:399
  38.1 2.2 %store.1 = (bf16[4096,256]{1,0:T(8,128)(2,1)}, bf16[256,256]{1,0:T(8,128)(2,1)}, f32[9,256,256]{2,1,0:T(8,128)}) custom-call(bf16[4096,256]{1,0:T(8,128)(2,1)S(1)} %get-tuple-element.9.gf_ref, bf16[256,256]{1,0:T(8,128)(2,1)S(1)} %get-tuple-element.10.gc_ref, f32[9,256,256]{2,1,0:T(8,128)S(1)} %get-tuple-element.11.gw_ref), custom_call_target="tpu_custom_call" | custom-call | tf_op jit(solution)/shard_map/store/pallas_call | solution.py:459
